TPU v7x, 32 devices: a whole 2x2x4 slice. The times are simulated.
32 devices in a mesh: section: 2 (over x), ctx: 8 (over z, core), tp: 2 (over y).
Axes of the slice: x: 2, y: 2, z: 4, core: 2. Of those that a mesh axis runs over, the one named last changes fastest.
Arguments:
- inputs: bfloat16 [2, 1024, 1024], P(None, 'ctx'), may hold values from -6 to 6
- cotangent: bfloat16 [2, 1024, 1024], P(None, 'ctx'), may hold values from -6 to 6
- ln1_gain: bfloat16 [2, 1024], P('section'), may hold values from 0.25 to 1.75
- ln1_bias: bfloat16 [2, 1024], P('section'), may hold values from -1.75 to 1.75
- ln2_gain: bfloat16 [2, 1024], P('section'), may hold values from 0.25 to 1.75
- ln2_bias: bfloat16 [2, 1024], P('section'), may hold values from -1.75 to 1.75
- qkv_weight: bfloat16 [2, 3, 1024, 1024], P('section', None, None, 'tp'), may hold values from -0.1875 to 0.1875
- qkv_bias: bfloat16 [2, 3, 1024], P('section', None, 'tp'), may hold values from -3 to 3
- out_weight: bfloat16 [2, 1024, 1024], P('section', 'tp'), may hold values from -0.75 to 0.75
- up_weight: bfloat16 [2, 1024, 4096], P('section', None, 'tp'), may hold values from -0.1875 to 0.1875
- up_bias: bfloat16 [2, 4096], P('section', 'tp'), may hold values from -3 to 3
- down_weight: bfloat16 [2, 4096, 1024], P('section', 'tp'), may hold values from -0.09375 to 0.09375
- branch_bias: bfloat16 [2, 1024], P('section'), may hold values from -3 to 3
Outputs:
- acts: bfloat16 [2, 2, 1024, 1024], P('section', None, 'ctx')
- in_grads: bfloat16 [2, 2, 1024, 1024], P('section', None, 'ctx')
- ln1_gain_grad: float32 [2, 1024], P('section')
- ln1_bias_grad: float32 [2, 1024], P('section')
- ln2_gain_grad: float32 [2, 1024], P('section')
- ln2_bias_grad: float32 [2, 1024], P('section')
- qkv_weight_grad: float32 [2, 3, 1024, 1024], P('section', None, 'ctx', 'tp')
- qkv_bias_grad: float32 [2, 3, 1024], P('section', None, 'tp')
- out_weight_grad: float32 [2, 1024, 1024], P('section', 'tp', 'ctx')
- up_weight_grad: float32 [2, 1024, 4096], P('section', 'ctx', 'tp')
- up_bias_grad: float32 [2, 4096], P('section', 'tp')
- down_weight_grad: float32 [2, 4096, 1024], P('section', 'tp', 'ctx')
- branch_bias_grad: float32 [2, 1024], P('section')
All inputs are finite; a program needn't handle non-finite values.
Results may differ from a plain program's by a relative error of at most 0.015.
Values may be sent and summed in bfloat16 or wider, within the bound.
No kernel may reach another device: no remote copies, remote signals or barrier semaphores. Data moves between devices by JAX's collectives and lax.ppermute only.
A program may use at most 320 MiB of HBM per device.

v0:
```python
import math

import jax
import jax.numpy as jnp
from jax import lax
from jax.sharding import PartitionSpec as P

HD = 64
ROT = 16


def shifted(shard, axis, by):
    peers = lax.axis_size(axis)
    pairs = [(i, i + by) for i in range(peers) if 0 <= i + by < peers]
    return lax.ppermute(shard, axis, pairs)


def tables(positions):
    freqs = 1.0 / 10000.0 ** (jnp.arange(0, ROT, 2).astype(jnp.float32) / ROT)
    angles = positions.astype(jnp.float32)[:, None] * freqs[None, :]
    return (jnp.cos(angles)[:, None, :], jnp.sin(angles)[:, None, :])


def rotate(field, cosine, sine):
    half_rot = ROT // 2
    front = field[..., :half_rot]
    second = field[..., half_rot:ROT]
    return jnp.concatenate(
        [front * cosine - second * sine, second * cosine + front * sine, field[..., ROT:]], axis=-1
    )


def norms(hidden, gain_one, shift_one, gain_two, shift_two):
    centre = hidden - jnp.mean(hidden, axis=-1, keepdims=True)
    normed = centre * lax.rsqrt(jnp.mean(centre * centre, axis=-1, keepdims=True) + 1e-05)
    return (normed * gain_one + shift_one, normed * gain_two + shift_two)


def gelu_exact(value):
    return jax.nn.gelu(value, approximate=False)


def scores_of(queries, keys, query_pos, score_scale):
    raw = jnp.einsum("qhd,khd->hqk", queries, keys, preferred_element_type=jnp.float32)
    key_pos = jnp.arange(keys.shape[0], dtype=jnp.int32)
    return jnp.where(
        key_pos[None, None, :] <= query_pos[None, :, None], raw * score_scale, -1000000000.0
    )


def forward_layer(layer_in, weights, query_pos, cosine, sine):
    gains, w_qkv, b_qkv, w_out, w_up, b_up, w_down, b_branch = weights
    hidden = layer_in.astype(jnp.float32)
    attn_norm, mlp_norm = norms(hidden, gains[0], gains[1], gains[2], gains[3])
    attn_in = attn_norm.astype(jnp.bfloat16)
    mlp_in = mlp_norm.astype(jnp.bfloat16)
    projected = (
        jnp.einsum("td,cdf->tcf", attn_in, w_qkv, preferred_element_type=jnp.float32) + b_qkv
    )
    row_count = hidden.shape[0]
    feat_width = projected.shape[2]
    head_count = feat_width // HD
    queries = rotate(projected[:, 0].reshape(row_count, head_count, HD), cosine, sine).astype(
        jnp.bfloat16
    )
    key_flat = (
        rotate(projected[:, 1].reshape(row_count, head_count, HD), cosine, sine)
        .astype(jnp.bfloat16)
        .reshape(row_count, feat_width)
    )
    value_flat = projected[:, 2].astype(jnp.bfloat16)
    all_keys, all_values = (
        lax.all_gather(key_flat, "ctx", axis=0, tiled=True),
        lax.all_gather(value_flat, "ctx", axis=0, tiled=True),
    )
    key_count = all_keys.shape[0]
    score_scale = 1.0 / math.sqrt(HD)
    scores = scores_of(queries, all_keys.reshape(key_count, head_count, HD), query_pos, score_scale)
    row_max = jnp.max(scores, axis=-1, keepdims=True)
    exponent = jnp.exp(scores - row_max)
    summed = jnp.sum(exponent, axis=-1, keepdims=True)
    probability = (exponent / summed).astype(jnp.bfloat16)
    log_total = row_max + jnp.log(summed)
    mixed = jnp.einsum(
        "hqk,khd->qhd",
        probability,
        all_values.reshape(key_count, head_count, HD),
        preferred_element_type=jnp.float32,
    )
    mixed = mixed.reshape(row_count, feat_width).astype(jnp.bfloat16)
    partial_out = jnp.dot(mixed, w_out, preferred_element_type=jnp.float32)
    up_value = jnp.dot(mlp_in, w_up, preferred_element_type=jnp.float32) + b_up
    active = gelu_exact(up_value).astype(jnp.bfloat16)
    partial_out = partial_out + jnp.dot(active, w_down, preferred_element_type=jnp.float32)
    branches = lax.psum(partial_out, "tp")
    layer_out = (hidden + branches + b_branch).astype(jnp.bfloat16)
    stored = (key_flat, value_flat)
    saved = (layer_in, queries, stored, log_total, mixed, up_value, active)
    return (layer_out, saved)


def backward_layer(grad_out, saved, weights, query_pos, cosine, sine):
    gains, w_qkv, b_qkv, w_out, w_up, b_up, w_down, b_branch = weights
    layer_in, queries, stored, log_total, mixed, up_value, active = saved
    grad_full = grad_out.astype(jnp.float32)
    row_count, feat_width = mixed.shape
    head_count = feat_width // HD
    hidden = layer_in.astype(jnp.float32)
    norm_pair, norm_back = jax.vjp(norms, hidden, gains[0], gains[1], gains[2], gains[3])
    attn_in = norm_pair[0].astype(jnp.bfloat16)
    mlp_in = norm_pair[1].astype(jnp.bfloat16)
    active_grad = jnp.einsum("td,fd->tf", grad_out, w_down, preferred_element_type=jnp.float32)
    grad_down = jnp.einsum("tf,td->fd", active, grad_out, preferred_element_type=jnp.float32)
    gelu_back = jax.vjp(gelu_exact, up_value)[1]
    up_grad = gelu_back(active_grad)[0].astype(jnp.bfloat16)
    grad_up_bias = jnp.sum(up_grad.astype(jnp.float32), axis=0)
    grad_up = jnp.einsum("td,tf->df", mlp_in, up_grad, preferred_element_type=jnp.float32)
    mlp_in_grad = jnp.einsum("tf,df->td", up_grad, w_up, preferred_element_type=jnp.float32)
    mixed_grad = jnp.einsum(
        "td,fd->tf", grad_out, w_out, preferred_element_type=jnp.float32
    ).astype(jnp.bfloat16)
    grad_out_weight = jnp.einsum("tf,td->fd", mixed, grad_out, preferred_element_type=jnp.float32)
    all_keys, all_values = (
        lax.all_gather(stored[0], "ctx", axis=0, tiled=True),
        lax.all_gather(stored[1], "ctx", axis=0, tiled=True),
    )
    key_count = all_keys.shape[0]
    keys_heads = all_keys.reshape(key_count, head_count, HD)
    values_heads = all_values.reshape(key_count, head_count, HD)
    score_scale = 1.0 / math.sqrt(HD)
    scores = scores_of(queries, keys_heads, query_pos, score_scale)
    probability = jnp.exp(scores - log_total)
    heads_grad = mixed_grad.reshape(row_count, head_count, HD)
    prob_grad = jnp.einsum(
        "qhd,khd->hqk", heads_grad, values_heads, preferred_element_type=jnp.float32
    )
    centre = jnp.sum(probability * prob_grad, axis=-1, keepdims=True)
    score_grad = (score_scale * probability * (prob_grad - centre)).astype(jnp.bfloat16)
    query_grad = jnp.einsum(
        "hqk,khd->qhd", score_grad, keys_heads, preferred_element_type=jnp.float32
    )
    value_terms = jnp.einsum(
        "hqk,qhd->khd",
        probability.astype(jnp.bfloat16),
        heads_grad,
        preferred_element_type=jnp.float32,
    )
    key_terms = jnp.einsum("hqk,qhd->khd", score_grad, queries, preferred_element_type=jnp.float32)
    key_grad, value_grad = (
        lax.psum_scatter(
            key_terms.reshape(key_count, feat_width), "ctx", scatter_dimension=0, tiled=True
        ),
        lax.psum_scatter(
            value_terms.reshape(key_count, feat_width), "ctx", scatter_dimension=0, tiled=True
        ),
    )
    query_grad = rotate(query_grad, cosine, -sine).reshape(row_count, feat_width)
    key_grad = rotate(key_grad.reshape(row_count, head_count, HD), cosine, -sine).reshape(
        row_count, feat_width
    )
    qkv_grad = jnp.stack([query_grad, key_grad, value_grad], axis=1).astype(jnp.bfloat16)
    grad_qkv_bias = jnp.sum(qkv_grad.astype(jnp.float32), axis=0)
    grad_qkv = jnp.einsum("td,tcf->cdf", attn_in, qkv_grad, preferred_element_type=jnp.float32)
    attn_in_grad = jnp.einsum("tcf,cdf->td", qkv_grad, w_qkv, preferred_element_type=jnp.float32)
    attn_in_grad, mlp_in_grad = lax.psum((attn_in_grad, mlp_in_grad), "tp")
    hidden_grad, gain_one_grad, shift_one_grad, gain_two_grad, shift_two_grad = norm_back(
        (attn_in_grad, mlp_in_grad)
    )
    input_grad = (grad_full + hidden_grad).astype(jnp.bfloat16)
    grad_branch = jnp.sum(grad_full, axis=0)
    grads = (
        gain_one_grad,
        shift_one_grad,
        gain_two_grad,
        shift_two_grad,
        grad_qkv,
        grad_qkv_bias,
        grad_out_weight,
        grad_up,
        grad_up_bias,
        grad_down,
        grad_branch,
    )
    return (input_grad, grads)


def per_device(
    inputs,
    cotangent,
    ln1_gain,
    ln1_bias,
    ln2_gain,
    ln2_bias,
    qkv_weight,
    qkv_bias,
    out_weight,
    up_weight,
    up_bias,
    down_weight,
    branch_bias,
):
    gains = (
        ln1_gain[0].astype(jnp.float32),
        ln1_bias[0].astype(jnp.float32),
        ln2_gain[0].astype(jnp.float32),
        ln2_bias[0].astype(jnp.float32),
    )
    weights = (
        gains,
        qkv_weight[0],
        qkv_bias[0].astype(jnp.float32),
        out_weight[0],
        up_weight[0],
        up_bias[0].astype(jnp.float32),
        down_weight[0],
        branch_bias[0].astype(jnp.float32),
    )
    micro_count = inputs.shape[0]
    row_count = inputs.shape[1]
    query_pos = lax.axis_index("ctx") * row_count + jnp.arange(row_count, dtype=jnp.int32)
    cosine, sine = tables(query_pos)
    at_first = lax.axis_index("section") == 0
    blank = jnp.zeros_like(inputs[0])
    received = blank
    outputs_list = []
    saved_list = []
    for step_index in range(micro_count + 1):
        fresh = inputs[step_index] if step_index < micro_count else blank
        layer_in = jnp.where(at_first, fresh, received)
        layer_out, saved = forward_layer(layer_in, weights, query_pos, cosine, sine)
        outputs_list.append(layer_out)
        saved_list.append(saved)
        if step_index < micro_count:
            received = shifted(layer_out, "section", 1)
    returned = blank
    grad_list = []
    sums = None
    for back_index in range(micro_count + 1):
        batch_index = micro_count - 1 - back_index
        given = cotangent[batch_index] if batch_index >= 0 else blank
        grad_in = jnp.where(at_first, returned, given)
        input_grad, grads = backward_layer(
            grad_in, saved_list[micro_count - back_index], weights, query_pos, cosine, sine
        )
        sums = grads if sums is None else jax.tree.map(jnp.add, sums, grads)
        grad_list.append(input_grad)
        if back_index < micro_count:
            returned = shifted(input_grad, "section", -1)
    acts = jnp.stack(
        [jnp.where(at_first, outputs_list[j], outputs_list[j + 1]) for j in range(micro_count)]
    )[None]
    in_grads = jnp.stack(
        [
            jnp.where(at_first, grad_list[micro_count - j], grad_list[micro_count - 1 - j])
            for j in range(micro_count)
        ]
    )[None]
    (
        gain_one_grad,
        shift_one_grad,
        gain_two_grad,
        shift_two_grad,
        grad_qkv,
        grad_qkv_bias,
        grad_out_weight,
        grad_up,
        grad_up_bias,
        grad_down,
        grad_branch,
    ) = sums
    qkv_part, out_part, up_part, down_part = (
        lax.psum_scatter(
            grad_qkv[None].astype(jnp.bfloat16), "ctx", scatter_dimension=2, tiled=True
        ).astype(jnp.float32),
        lax.psum_scatter(
            grad_out_weight[None].astype(jnp.bfloat16), "ctx", scatter_dimension=2, tiled=True
        ).astype(jnp.float32),
        lax.psum_scatter(
            grad_up[None].astype(jnp.bfloat16), "ctx", scatter_dimension=1, tiled=True
        ).astype(jnp.float32),
        lax.psum_scatter(
            grad_down[None].astype(jnp.bfloat16), "ctx", scatter_dimension=2, tiled=True
        ).astype(jnp.float32),
    )
    small_sums = (
        lax.psum(gain_one_grad[None].astype(jnp.bfloat16), "ctx").astype(jnp.float32),
        lax.psum(shift_one_grad[None].astype(jnp.bfloat16), "ctx").astype(jnp.float32),
        lax.psum(gain_two_grad[None].astype(jnp.bfloat16), "ctx").astype(jnp.float32),
        lax.psum(shift_two_grad[None].astype(jnp.bfloat16), "ctx").astype(jnp.float32),
        lax.psum(grad_qkv_bias[None].astype(jnp.bfloat16), "ctx").astype(jnp.float32),
        lax.psum(grad_up_bias[None].astype(jnp.bfloat16), "ctx").astype(jnp.float32),
        lax.psum(grad_branch[None].astype(jnp.bfloat16), "ctx").astype(jnp.float32),
    )
    return (
        acts,
        in_grads,
        small_sums[0],
        small_sums[1],
        small_sums[2],
        small_sums[3],
        qkv_part,
        small_sums[4],
        out_part,
        up_part,
        small_sums[5],
        down_part,
        small_sums[6],
    )


def solution(mesh):
    placed = (
        P(None, "ctx", None),
        P(None, "ctx", None),
        P("section", None),
        P("section", None),
        P("section", None),
        P("section", None),
        P("section", None, None, "tp"),
        P("section", None, "tp"),
        P("section", "tp", None),
        P("section", None, "tp"),
        P("section", "tp"),
        P("section", "tp", None),
        P("section", None),
    )
    return jax.shard_map(
        per_device,
        mesh=mesh,
        in_specs=placed,
        out_specs=(
            P("section", None, "ctx", None),
            P("section", None, "ctx", None),
            P("section", None),
            P("section", None),
            P("section", None),
            P("section", None),
            P("section", None, "ctx", "tp"),
            P("section", None, "tp"),
            P("section", "tp", "ctx"),
            P("section", "ctx", "tp"),
            P("section", "tp"),
            P("section", "tp", "ctx"),
            P("section", None),
        ),
        check_vma=False,
    )
```

profile of v0, /device:TPU:0, one launch (start us, length us, event | category | flops | bytes accessed | tf_op | source)
XLA Modules:
  0.0 896.3 jit_solution(11353639533566223050)
XLA Ops:
  29.6 3.6 fusion.10
  33.2 14.5 %all-gather.10.cloned.1.call-done = bf16[1024,512]{0,1:T(8,128)(2,1)} async-done(((bf16[128,512]{0,1:T(8,128)(2,1)}), bf16[1024,512]{0,1:T(8,128)(2,1)}) %all-gather.10.cloned.1.call-update) | async-done | bytes 1048592 | tf_op jit(solution)/shard_map/all_gather | solution.py:73
  53.0 17.8 %all-gather.16.cloned.1.call-done = bf16[1024,1,512]{2,0,1:T(8,128)(2,1)} async-done(((bf16[128,1,512]{2,0,1:T(8,128)(2,1)}), bf16[1024,1,512]{2,0,1:T(8,128)(2,1)}) %all-gather.16.cloned.1.call-update) | async-done | bytes 1048592 | tf_op jit(solution)/shard_map/all_gather | solution.py:74
  73.1 3.6 fusion.87
  78.6 28.3 %all-reduce.10.cloned.1.call-done = f32[128,1024]{1,0:T(8,128)} async-done(((f32[128,1024]{1,0:T(8,128)}), f32[128,1024]{1,0:T(8,128)}) %all-reduce.10.cloned.1.call-update) | async-done | bytes 524304 | tf_op jit(solution)/shard_map/psum | solution.py:95
  108.1 3.4 collective-permute-start
  111.5 5.5 collective-permute-done
  133.8 6.2 multiply_convert_fusion.4
  142.4 13.1 %all-gather.12.cloned.1.call-done = bf16[1024,512]{0,1:T(8,128)(2,1)} async-done(((bf16[128,512]{0,1:T(8,128)(2,1)}), bf16[1024,512]{0,1:T(8,128)(2,1)}) %all-gather.12.cloned.1.call-update) | async-done | bytes 1048592 | tf_op jit(solution)/shard_map/all_gather | solution.py:73
  161.5 16.3 %all-gather.18.cloned.1.call-done = bf16[1024,1,512]{2,0,1:T(8,128)(2,1)} async-done(((bf16[128,1,512]{2,0,1:T(8,128)(2,1)}), bf16[1024,1,512]{2,0,1:T(8,128)(2,1)}) %all-gather.18.cloned.1.call-update) | async-done | bytes 1048592 | tf_op jit(solution)/shard_map/all_gather | solution.py:74
  180.0 3.6 fusion.86
  185.5 28.3 %all-reduce.12.cloned.1.call-done = f32[128,1024]{1,0:T(8,128)} async-done(((f32[128,1024]{1,0:T(8,128)}), f32[128,1024]{1,0:T(8,128)}) %all-reduce.12.cloned.1.call-update) | async-done | bytes 524304 | tf_op jit(solution)/shard_map/psum | solution.py:95
  215.8 3.3 collective-permute-start.1
  219.1 5.5 collective-permute-done.1
  244.5 17.5 %all-gather.14.cloned.1.call-done = bf16[1024,512]{0,1:T(8,128)(2,1)} async-done(((bf16[128,512]{0,1:T(8,128)(2,1)}), bf16[1024,512]{0,1:T(8,128)(2,1)}) %all-gather.14.cloned.1.call-update) | async-done | bytes 1048592 | tf_op jit(solution)/shard_map/all_gather | solution.py:73
  268.7 16.2 %all-gather.20.cloned.1.call-done = bf16[1024,1,512]{2,0,1:T(8,128)(2,1)} async-done(((bf16[128,1,512]{2,0,1:T(8,128)(2,1)}), bf16[1024,1,512]{2,0,1:T(8,128)(2,1)}) %all-gather.20.cloned.1.call-update) | async-done | bytes 1048592 | tf_op jit(solution)/shard_map/all_gather | solution.py:74
  287.2 3.9 multiply_reduce_fusion.2
  295.4 4.5 fusion.58
  303.1 3.2 fusion.51
  306.6 4.3 convert_reduce_fusion.2
  315.5 15.5 %reduce-scatter.17.cloned.1.call-done = f32[128,512]{0,1:T(8,128)} async-done(((f32[1024,512]{0,1:T(8,128)}), f32[128,512]{0,1:T(8,128)}) %reduce-scatter.17.cloned.1.call-update) | async-done | bytes 262160 | tf_op jit(solution)/shard_map/reduce_scatter | solution.py:150
  338.4 29.1 %reduce-scatter.19.cloned.1.call-done = f32[128,512]{1,0:T(8,128)} async-done(((f32[1024,512]{1,0:T(8,128)}), f32[128,512]{1,0:T(8,128)}) %reduce-scatter.19.cloned.1.call-update) | async-done | bytes 262160 | tf_op jit(solution)/shard_map/reduce_scatter | solution.py:153
  372.0 39.0 %all-reduce.18.cloned.1.call-done = (f32[128,1024]{1,0:T(8,128)}, f32[128,1024]{1,0:T(8,128)}) async-done(((f32[128,1024]{1,0:T(8,128)}, f32[128,1024]{1,0:T(8,128)}), (f32[128,1024]{1,0:T(8,128)}, f32[128,1024]{1,0:T(8,128)})) %all-reduce.18.cloned.1.call-update) | async-done | bytes 1048592 | tf_op jit(solution)/shard_map/psum | solution.py:165
  418.9 7.6 collective-permute-done.2
  430.2 3.9 multiply_reduce_fusion.1
  438.4 4.4 fusion.56
  449.4 7.0 convert_reduce_fusion.1
  459.5 13.8 %reduce-scatter.21.cloned.1.call-done = f32[128,512]{0,1:T(8,128)} async-done(((f32[1024,512]{0,1:T(8,128)}), f32[128,512]{0,1:T(8,128)}) %reduce-scatter.21.cloned.1.call-update) | async-done | bytes 262160 | tf_op jit(solution)/shard_map/reduce_scatter | solution.py:150
  480.7 29.5 %reduce-scatter.23.cloned.1.call-done = f32[128,512]{1,0:T(8,128)} async-done(((f32[1024,512]{1,0:T(8,128)}), f32[128,512]{1,0:T(8,128)}) %reduce-scatter.23.cloned.1.call-update) | async-done | bytes 262160 | tf_op jit(solution)/shard_map/reduce_scatter | solution.py:153
  514.7 39.0 %all-reduce.16.cloned.1.call-done = (f32[128,1024]{1,0:T(8,128)}, f32[128,1024]{1,0:T(8,128)}) async-done(((f32[128,1024]{1,0:T(8,128)}, f32[128,1024]{1,0:T(8,128)}), (f32[128,1024]{1,0:T(8,128)}, f32[128,1024]{1,0:T(8,128)})) %all-reduce.16.cloned.1.call-update) | async-done | bytes 1048592 | tf_op jit(solution)/shard_map/psum | solution.py:165
  562.3 7.8 collective-permute-done.3
  573.1 3.9 multiply_reduce_fusion
  581.3 4.5 fusion.54
  588.9 8.0 fusion.197
  606.7 6.0 copy.130
  615.9 6.9 convert_reduce_fusion
  630.7 22.2 %reduce-scatter.27.cloned.1.call-done = f32[128,512]{1,0:T(8,128)} async-done(((f32[1024,512]{1,0:T(8,128)}), f32[128,512]{1,0:T(8,128)}) %reduce-scatter.27.cloned.1.call-update) | async-done | bytes 262160 | tf_op jit(solution)/shard_map/reduce_scatter | solution.py:153
  659.4 7.3 fusion.28
  666.7 20.6 %copy.132 = bf16[1,2048,1024]{1,0,2:T(2,128)(2,1)} copy(bf16[1,2048,1024]{2,1,0:T(8,128)(2,1)} %fusion.28) | data formatting | bytes 8388608
  687.3 8.1 copy.139
  700.1 3.4 fusion.27
  710.4 7.7 copy.128
  718.1 5.1 copy.136
  742.9 31.7 %all-reduce.3 = (bf16[1,1024]{1,0:T(2,128)(2,1)S(1)}, bf16[1,1024]{1,0:T(2,128)(2,1)S(1)}, bf16[1,1024]{1,0:T(2,128)(2,1)S(1)}, bf16[1,1024]{1,0:T(2,128)(2,1)S(...) all-reduce(bf16[1,1024]{1,0:T(2,128)(2,1)S(1)} %convert_element_typ, ...), channel_id=1, replica_groups=mesh['section'=2,'ctx'=8,'tp'=2] {'ctx'}, use_global_device_ids=true, to_apply=%region_39.40 | all-reduce | flops 8704 | bytes 34816 | tf_op jit(solution)/shard_map/psum | solution.py:286
  784.2 9.1 %reduce-scatter.35.cloned.1.call-done = bf16[128,2048]{1,0:T(8,128)(2,1)} async-done(((bf16[1024,2048]{1,0:T(8,128)(2,1)}), bf16[128,2048]{1,0:T(8,128)(2,1)}) %reduce-scatter.35.cloned.1.call-update) | async-done | bytes 524304
  795.9 3.5 copy.133
  801.5 42.1 %reduce-scatter.29.cloned.1.call-done = bf16[1,128,2048]{2,1,0:T(8,128)(2,1)} async-done(((bf16[1,1024,2048]{2,1,0:T(8,128)(2,1)}), bf16[1,128,2048]{2,1,0:T(8,128)(2,1)}) %reduce-scatter.29.cloned.1.call-update) | async-done | bytes 524304 | tf_op jit(solution)/shard_map/reduce_scatter | solution.py:278
  845.7 38.8 %reduce-scatter.31.cloned.1.call-done = bf16[128,1536]{1,0:T(8,128)(2,1)} async-done(((bf16[1024,1536]{1,0:T(8,128)(2,1)}), bf16[128,1536]{1,0:T(8,128)(2,1)}) %reduce-scatter.31.cloned.1.call-update) | async-done | bytes 393232
  (497 shorter events, 252.1 us)
Async XLA Ops:
  7.2 40.5 %all-gather.10.cloned.1.call-start = ((), (), s32[]{:S(2)}) async-start(), calls=%async_computation.10 | async-start | bytes 1179648 | tf_op jit(solution)/shard_map/all_gather | solution.py:73
  20.2 27.5 %copy-start.85 = (bf16[128,8,8]{0,2,1:T(8,128)(2,1)}, bf16[128,8,8]{0,2,1:T(8,128)(2,1)S(1)}, u32[]{:S(2)}) copy-start(bf16[128,8,8]{0,2,1:T(8,128)(2,1)S(1)} %get-tuple-element.122) | copy-start | bytes 49156
  20.2 27.5 %copy-start.87 = (bf16[128,8,8]{0,2,1:T(8,128)(2,1)}, bf16[128,8,8]{0,2,1:T(8,128)(2,1)S(1)}, u32[]{:S(2)}) copy-start(bf16[128,8,8]{0,2,1:T(8,128)(2,1)S(1)} %get-tuple-element.123) | copy-start | bytes 49156
  20.9 49.9 %all-gather.16.cloned.1.call-start = ((), (), s32[]{:S(2)}) async-start(), calls=%async_computation.22 | async-start | bytes 1179648 | tf_op jit(solution)/shard_map/all_gather | solution.py:74
  22.6 84.4 %all-reduce.10.cloned.1.call-start = ((), (), s32[]{:S(2)}) async-start(), calls=%async_computation.11 | async-start | bytes 1048576 | tf_op jit(solution)/shard_map/psum | solution.py:95
  23.5 9.7 %copy-start.94 = (f32[1,2048]{1,0:T(1,128)}, f32[1,2048]{1,0:T(1,128)S(1)}, u32[]{:S(2)}) copy-start(f32[1,2048]{1,0:T(1,128)S(1)} %add.611) | copy-start | bytes 24580
  29.4 18.3 %copy-start.71 = (bf16[128,8,48]{0,2,1:T(8,128)(2,1)}, bf16[128,8,48]{0,2,1:T(8,128)(2,1)S(1)}, u32[]{:S(2)}) copy-start(bf16[128,8,48]{0,2,1:T(8,128)(2,1)S(1)} %slice.379) | copy-start | bytes 294916
  49.9 26.8 %copy-start.103 = (f32[8,128]{1,0:T(8,128)}, f32[8,128]{1,0:T(8,128)S(1)}, u32[]{:S(2)}) copy-start(f32[8,128]{1,0:T(8,128)S(1)} %get-tuple-element.141) | copy-start | bytes 12292
  53.0 23.7 %copy-start.126 = (f32[8,128]{1,0:T(8,128)}, f32[8,128]{1,0:T(8,128)S(1)}, u32[]{:S(2)}) copy-start(f32[8,128]{1,0:T(8,128)S(1)} %fusion.24) | copy-start | bytes 12292
  78.6 76.9 %all-gather.12.cloned.1.call-start = ((), (), s32[]{:S(2)}) async-start(), calls=%async_computation.12 | async-start | bytes 1179648 | tf_op jit(solution)/shard_map/all_gather | solution.py:73
  78.6 32.9 %copy-start.96 = (f32[1,1024]{1,0:T(1,128)}, f32[1,1024]{1,0:T(1,128)S(1)}, u32[]{:S(2)}) copy-start(f32[1,1024]{1,0:T(1,128)S(1)} %add.612) | copy-start | bytes 12292
  108.1 10.3 %copy-start.70 = (bf16[128,1024]{1,0:T(8,128)(2,1)}, bf16[128,1024]{1,0:T(8,128)(2,1)S(1)}, u32[]{:S(2)}) copy-start(bf16[128,1024]{1,0:T(8,128)(2,1)S(1)} %fusion.156) | copy-start | bytes 786436
  108.1 8.9 collective-permute-start
  118.2 95.7 %copy-start.16 = (bf16[128,1024]{1,0:T(8,128)(2,1)}, bf16[128,1024]{1,0:T(8,128)(2,1)S(1)}, u32[]{:S(2)}) copy-start(bf16[128,1024]{1,0:T(8,128)(2,1)S(1)} %get-tuple-element.94) | copy-start | bytes 786436
  130.3 47.5 %all-gather.18.cloned.1.call-start = ((), (), s32[]{:S(2)}) async-start(), calls=%async_computation.23 | async-start | bytes 1179648 | tf_op jit(solution)/shard_map/all_gather | solution.py:74
  133.6 80.3 %all-reduce.12.cloned.1.call-start = ((), (), s32[]{:S(2)}) async-start(), calls=%async_computation.13 | async-start | bytes 1048576 | tf_op jit(solution)/shard_map/psum | solution.py:95
  185.5 76.5 %all-gather.14.cloned.1.call-start = ((), (), s32[]{:S(2)}) async-start(), calls=%async_computation.14 | async-start | bytes 1179648 | tf_op jit(solution)/shard_map/all_gather | solution.py:73
  215.8 9.2 %copy-start.65 = (bf16[128,1024]{1,0:T(8,128)(2,1)}, bf16[128,1024]{1,0:T(8,128)(2,1)S(1)}, u32[]{:S(2)}) copy-start(bf16[128,1024]{1,0:T(8,128)(2,1)S(1)} %get-tuple-element.88) | copy-start | bytes 786436
  215.8 8.8 collective-permute-start.1
  236.8 48.1 %all-gather.20.cloned.1.call-start = ((), (), s32[]{:S(2)}) async-start(), calls=%async_computation.24 | async-start | bytes 1179648 | tf_op jit(solution)/shard_map/all_gather | solution.py:74
  238.5 92.4 %reduce-scatter.17.cloned.1.call-start = ((), (), s32[]{:S(2)}) async-start(), calls=%async_computation.15 | async-start | bytes 2359296 | tf_op jit(solution)/shard_map/reduce_scatter | solution.py:150
  264.3 22.9 %copy-start.60 = (bf16[128,512]{0,1:T(8,128)(2,1)S(1)}, bf16[128,512]{0,1:T(8,128)(2,1)}, u32[]{:S(2)}) copy-start(bf16[128,512]{0,1:T(8,128)(2,1)} %copy.109) | copy-start | bytes 393220
  295.4 72.1 %reduce-scatter.19.cloned.1.call-start = ((), (), s32[]{:S(2)}) async-start(), calls=%async_computation.16 | async-start | bytes 2359296 | tf_op jit(solution)/shard_map/reduce_scatter | solution.py:153
  303.0 108.0 %all-reduce.18.cloned.1.call-start = ((), (), s32[]{:S(2)}) async-start(), calls=%async_computation.30 | async-start | bytes 2097152 | tf_op jit(solution)/shard_map/psum | solution.py:165
  335.1 80.4 %copy-start.50 = (bf16[128,1,512]{2,0,1:T(8,128)(2,1)}, bf16[128,1,512]{2,0,1:T(8,128)(2,1)S(1)}, u32[]{:S(2)}) copy-start(bf16[128,1,512]{2,0,1:T(8,128)(2,1)S(1)} %copy.112) | copy-start | bytes 393220
  372.0 101.3 %reduce-scatter.21.cloned.1.call-start = ((), (), s32[]{:S(2)}) async-start(), calls=%async_computation.17 | async-start | bytes 2359296 | tf_op jit(solution)/shard_map/reduce_scatter | solution.py:150
  411.0 15.5 %copy-start.58 = (bf16[2,128,1024]{2,1,0:T(8,128)(2,1)S(1)}, bf16[2,128,1024]{2,1,0:T(8,128)(2,1)}, u32[]{:S(2)}) copy-start(bf16[2,128,1024]{2,1,0:T(8,128)(2,1)} %param.14) | copy-start | bytes 1572868
  411.0 17.0 %copy-start.13 = (bf16[1,512,1024]{2,1,0:T(8,128)(2,1)S(1)}, bf16[1,512,1024]{2,1,0:T(8,128)(2,1)}, u32[]{:S(2)}) copy-start(bf16[1,512,1024]{2,1,0:T(8,128)(2,1)} %param.21) | copy-start | bytes 3145732
  416.6 10.7 %copy-start.67 = (bf16[128,1024]{1,0:T(8,128)(2,1)}, bf16[128,1024]{1,0:T(8,128)(2,1)S(1)}, u32[]{:S(2)}) copy-start(bf16[128,1024]{1,0:T(8,128)(2,1)S(1)} %fusion.144) | copy-start | bytes 786436
  416.6 9.9 %collective-permute-start.2 = (bf16[128,1024]{1,0:T(8,128)(2,1)S(1)}, bf16[128,1024]{1,0:T(8,128)(2,1)S(1)}, u32[]{:S(2)}, u32[]{:S(2)}) collective-permute-start(bf16[128,1024]{1,0:T(8,128)(2,1)S(1)} %fusion.144), channel_id=1, source_target_pairs={{16,0},{17,1},{18,2},{19,3},{20,4},{21,5},{22,6},{23,7},{24,8},{25... | collective-permute-start | bytes 786440 | tf_op jit(solution)/shard_map/ppermute | solution.py:15
  438.3 71.9 %reduce-scatter.23.cloned.1.call-start = ((), (), s32[]{:S(2)}) async-start(), calls=%async_computation.18 | async-start | bytes 2359296 | tf_op jit(solution)/shard_map/reduce_scatter | solution.py:153
  445.8 108.0 %all-reduce.16.cloned.1.call-start = ((), (), s32[]{:S(2)}) async-start(), calls=%async_computation.29 | async-start | bytes 2097152 | tf_op jit(solution)/shard_map/psum | solution.py:165
  477.4 81.0 %copy-start.52 = (bf16[128,1,512]{2,0,1:T(8,128)(2,1)}, bf16[128,1,512]{2,0,1:T(8,128)(2,1)S(1)}, u32[]{:S(2)}) copy-start(bf16[128,1,512]{2,0,1:T(8,128)(2,1)S(1)} %copy.116) | copy-start | bytes 393220
  514.7 111.2 %reduce-scatter.25.cloned.1.call-start = ((), (), s32[]{:S(2)}) async-start(), calls=%async_computation.19 | async-start | bytes 2359296 | tf_op jit(solution)/shard_map/reduce_scatter | solution.py:150
  553.8 7.9 copy-start.127
  553.8 17.1 %copy-start.14 = (bf16[1,512,1024]{2,1,0:T(8,128)(2,1)S(1)}, bf16[1,512,1024]{2,1,0:T(8,128)(2,1)}, u32[]{:S(2)}) copy-start(bf16[1,512,1024]{2,1,0:T(8,128)(2,1)} %param.21) | copy-start | bytes 3145732
  560.3 9.9 %copy-start.66 = (bf16[128,1024]{1,0:T(8,128)(2,1)}, bf16[128,1024]{1,0:T(8,128)(2,1)S(1)}, u32[]{:S(2)}) copy-start(bf16[128,1024]{1,0:T(8,128)(2,1)S(1)} %get-tuple-element.86) | copy-start | bytes 786436
  560.3 9.9 %collective-permute-start.3 = (bf16[128,1024]{1,0:T(8,128)(2,1)S(1)}, bf16[128,1024]{1,0:T(8,128)(2,1)S(1)}, u32[]{:S(2)}, u32[]{:S(2)}) collective-permute-start(bf16[128,1024]{1,0:T(8,128)(2,1)S(1)} %get-tuple-element.86), channel_id=1, source_target_pairs={{16,0},{17,1},{18,2},{19,3},{20,4},{21,5},{22,6},{23,7},{24,8},{25... | collective-permute-start | bytes 786440 | tf_op jit(solution)/shard_map/ppermute | solution.py:15
  581.3 71.6 %reduce-scatter.27.cloned.1.call-start = ((), (), s32[]{:S(2)}) async-start(), calls=%async_computation.20 | async-start | bytes 2359296 | tf_op jit(solution)/shard_map/reduce_scatter | solution.py:153
  588.8 141.4 %reduce-scatter.33.cloned.1.call-start = ((), (), s32[]{:S(2)}) async-start(), calls=%async_computation.26 | async-start | bytes 1179648
  588.9 8.0 copy-start.31
  588.9 8.0 copy-start.64
  615.6 124.2 %all-reduce.14.cloned.1.call-start = ((), (), s32[]{:S(2)}) async-start(), calls=%async_computation.28 | async-start | bytes 3145728 | tf_op jit(solution)/shard_map/psum | solution.py:95
  656.8 136.5 %reduce-scatter.35.cloned.1.call-start = ((), (), s32[]{:S(2)}) async-start(), calls=%async_computation.27 | async-start | bytes 4718592
  695.4 148.2 %reduce-scatter.29.cloned.1.call-start = ((), (), s32[]{:S(2)}) async-start(), calls=%async_computation.21 | async-start | bytes 4718592 | tf_op jit(solution)/shard_map/reduce_scatter | solution.py:278
  703.5 181.1 %reduce-scatter.31.cloned.1.call-start = ((), (), s32[]{:S(2)}) async-start(), calls=%async_computation.25 | async-start | bytes 3538944
  723.2 57.9 %copy-start.97 = (f32[1,1024]{1,0:T(1,128)S(1)}, f32[1,1024]{1,0:T(1,128)}, u32[]{:S(2)}) copy-start(f32[1,1024]{1,0:T(1,128)} %copy-done.96) | copy-start | bytes 12292
  774.6 8.7 copy-start.69
  (112 other events, 310.8 us)
Sparse Core Ops, SparseCore 0:
  21.0 26.6 all-gather.9
  49.9 20.9 all-gather.15
  78.7 28.2 all-reduce.9
  130.4 24.9 all-gather.11
  157.0 20.7 all-gather.17
  185.6 28.2 all-reduce.11
  237.0 24.9 all-gather.13
  264.2 20.6 all-gather.19
  295.5 35.4 reduce-scatter.16
  333.1 34.3 reduce-scatter.18
  372.1 38.8 all-reduce.17
  438.4 34.8 reduce-scatter.20
  475.7 34.4 reduce-scatter.22
  514.8 38.9 all-reduce.15
  581.4 34.8 reduce-scatter.24
  618.4 34.4 reduce-scatter.26
  655.6 31.0 reduce-scatter.32
  689.6 50.1 all-reduce.13
  742.2 51.0 reduce-scatter.34
  795.5 48.0 reduce-scatter.28
  846.0 38.4 reduce-scatter.30
where the time goes:
time: 908 us; the launch traced here: 896 us
  waiting for transfers between devices  460 us (51%)
  matrix products  150 us (17%)
  local copies, waits for them, and re-layouts  147 us (16%)
  other arithmetic  80.8 us (9%)
  blocking collectives  31.7 us (3%)
  between operations  16.1 us (2%)
  starting transfers between devices  11.7 us (1%)
    unnamed x283, local copies, waits for them, and re-layouts  88.6 us
    reduce_scatter x3, waiting for transfers between devices, backward_layer(): lax.psum_scatter(value_terms.reshape(key_count, feat_width), 'ctx', scatt...  80.8 us
    psum x2, waiting for transfers between devices, backward_layer(): attn_in_grad, mlp_in_grad = lax.psum((attn_in_grad, mlp_in_grad), 'tp')  78 us
    psum x3, waiting for transfers between devices, forward_layer(): branches = lax.psum(partial_out, 'tp')  59.3 us
    all_gather x3, waiting for transfers between devices, forward_layer(): lax.all_gather(value_flat, 'ctx', axis=0, tiled=True)  50.3 us
    unnamed x24, waiting for transfers between devices  48.3 us
    all_gather x3, waiting for transfers between devices, forward_layer(): lax.all_gather(key_flat, 'ctx', axis=0, tiled=True)  45.1 us
    reduce_scatter x1, waiting for transfers between devices, per_device(): lax.psum_scatter(grad_up[None].astype(jnp.bfloat16), 'ctx', scatter_dimen...  42.1 us
  transfers between devices with their start and end apart: 25, of which 23 were waited for; matrix products, arithmetic and copies ran while one was open for 28% of the time, Pallas kernels for 0%

commit v1 on v0

--- a/solution.py
+++ b/solution.py
@@ -308,7 +308,390 @@
     )
 
 
-def solution(mesh):
+ALL = ("section", "ctx", "tp")
+SECTION, HALF, NEAR, CORE, SIDE = 16, 8, 4, 2, 1
+CHIPS = (0, SIDE, NEAR, NEAR | SIDE, SECTION, SECTION | SIDE, SECTION | NEAR, SECTION | NEAR | SIDE)
+
+
+def swapped(array, mask, only=None):
+    pairs = [(i, i ^ mask) for i in range(32) if only is None or only(i)]
+    return lax.ppermute(array, ALL, pairs)
+
+
+def pick(array, index, axis=0):
+    return lax.dynamic_index_in_dim(array, index, axis, keepdims=False)
+
+
+def part(array, index, size, axis):
+    return lax.dynamic_slice_in_dim(array, index * size, size, axis)
+
+
+def in_order(relative, index):
+    pieces = list(relative)
+    bit = 1
+    while bit < len(pieces):
+        flip = (index & bit) != 0
+        pieces = [jnp.where(flip, pieces[j ^ bit], pieces[j]) for j in range(len(pieces))]
+        bit *= 2
+    return jnp.stack(pieces)
+
+
+class Place:
+    def __init__(self):
+        self.section = lax.axis_index("section")
+        self.ctx = lax.axis_index("ctx")
+        self.side = lax.axis_index("tp")
+        self.half = self.ctx // 4
+        self.near = (self.ctx // 2) % 2
+        self.core = self.ctx % 2
+        self.chip = 4 * self.section + 2 * self.near + self.side
+
+
+def gather_start(array, at):
+    mine = pick(array, at.half)
+    other = pick(array, 1 - at.half)
+    width = other.shape[-1] // 2
+    strip = part(other, at.side, width, 1)
+    near = swapped(mine, NEAR)
+    far = jnp.stack([swapped(strip, HALF), swapped(strip, HALF | NEAR)])
+    rest = swapped(far, SIDE)
+    first = jnp.where(at.side == 0, far, rest)
+    second = jnp.where(at.side == 0, rest, far)
+    far = jnp.concatenate([first, second], axis=-1)
+    return in_order([mine, near, far[0], far[1]], 2 * at.half + at.near)
+
+
+def shard_weights(section_weights, at):
+    gains, w_qkv, b_qkv, w_out, w_up, b_up, w_down, b_branch = section_weights
+
+    def cut(index):
+        return (
+            part(w_qkv, index, w_qkv.shape[2] // 4, 2),
+            part(w_up, index, w_up.shape[1] // 4, 1),
+            part(w_out, index, w_out.shape[0] // 4, 0),
+            part(w_down, index, w_down.shape[0] // 4, 0),
+            jnp.concatenate(
+                list(gains)
+                + [b_branch]
+                + [part(b_qkv, index, b_qkv.shape[1] // 4, 1).reshape(-1)]
+                + [part(b_up, index, b_up.shape[0] // 4, 0)]
+            )[None],
+        )
+
+    own = cut(2 * at.section + at.near)
+    give = cut(2 * (1 - at.section) + at.near)
+
+    def exchange(array, axis):
+        size = array.shape[axis] // 2
+        got = swapped(part(array, at.core, size, axis), SECTION)
+        rest = swapped(got, CORE)
+        low = jnp.where(at.core == 0, got, rest)
+        high = jnp.where(at.core == 0, rest, got)
+        return jnp.concatenate([low, high], axis=axis)
+
+    taken = (
+        exchange(give[0], 1),
+        exchange(give[1], 0),
+        exchange(give[2], 0),
+        exchange(give[3], 0),
+        swapped(give[4], SECTION),
+    )
+    layers = []
+    for layer in range(2):
+        qkv, up, out, down, small = [
+            jnp.where(at.section == layer, a, b) for a, b in zip(own, taken)
+        ]
+        small = small[0].astype(jnp.float32)
+        dim = w_up.shape[0]
+        heads = qkv.shape[2]
+        layers.append(
+            dict(
+                gains=[small[i * dim : (i + 1) * dim] for i in range(4)],
+                branch=small[4 * dim : 5 * dim],
+                b_qkv=small[5 * dim : 5 * dim + 3 * heads].reshape(3, heads),
+                b_up=small[5 * dim + 3 * heads :],
+                qkv=qkv,
+                up=up,
+                out=out,
+                down=down,
+            )
+        )
+    return layers
+
+
+def turn(flat, cosine, sine):
+    rows, width = flat.shape
+    return rotate(flat.reshape(rows, width // HD, HD), cosine, sine).reshape(rows, width)
+
+
+def normal(x):
+    hidden = x.astype(jnp.float32)
+    centre = hidden - jnp.mean(hidden, axis=-1, keepdims=True)
+    scale = lax.rsqrt(jnp.mean(centre * centre, axis=-1, keepdims=True) + 1e-05)
+    return centre * scale, scale
+
+
+def forward_part(x, w, own_pos, other_pos, cosine, sine):
+    normed, _ = normal(x)
+    g = w["gains"]
+    attn_in = (normed * g[0] + g[1]).astype(jnp.bfloat16)
+    mlp_in = (normed * g[2] + g[3]).astype(jnp.bfloat16)
+    projected = (
+        jnp.einsum("td,cdf->ctf", attn_in, w["qkv"], preferred_element_type=jnp.float32)
+        + w["b_qkv"][:, None]
+    )
+    q = turn(projected[0], cosine, sine).astype(jnp.bfloat16)
+    k = turn(projected[1], cosine, sine).astype(jnp.bfloat16)
+    v = projected[2].astype(jnp.bfloat16)
+    kv = jnp.stack([k, v])
+    kv = jnp.concatenate([kv, swapped(kv, CORE)], axis=1)
+    rows, width = q.shape
+    heads = width // HD
+    keys = kv[0].reshape(-1, heads, HD)
+    values = kv[1].reshape(-1, heads, HD)
+    raw = jnp.einsum(
+        "qhd,khd->hqk", q.reshape(rows, heads, HD), keys, preferred_element_type=jnp.float32
+    )
+    key_pos = jnp.concatenate([own_pos, other_pos])
+    allowed = key_pos[None, None, :] <= own_pos[None, :, None]
+    scores = jnp.where(allowed, raw * (1.0 / math.sqrt(HD)), -1e9)
+    row_max = jnp.max(scores, axis=-1, keepdims=True)
+    exponent = jnp.exp(scores - row_max)
+    prob = exponent / jnp.sum(exponent, axis=-1, keepdims=True)
+    mixed = jnp.einsum(
+        "hqk,khd->qhd", prob.astype(jnp.bfloat16), values, preferred_element_type=jnp.float32
+    )
+    mixed = mixed.reshape(rows, width).astype(jnp.bfloat16)
+    up = jnp.dot(mlp_in, w["up"], preferred_element_type=jnp.float32) + w["b_up"]
+    active = gelu_exact(up).astype(jnp.bfloat16)
+    partial = jnp.dot(mixed, w["out"], preferred_element_type=jnp.float32) + jnp.dot(
+        active, w["down"], preferred_element_type=jnp.float32
+    )
+    saved = dict(
+        x=x, normed=normed, attn_in=attn_in, mlp_in=mlp_in, q=q, keys=keys, values=values,
+        prob=prob, mixed=mixed, up=up, active=active,
+    )
+    return partial, saved
+
+
+def backward_part(g, saved, w, cosine, sine):
+    f32 = jnp.float32
+    active_grad = jnp.einsum("td,fd->tf", g, w["down"], preferred_element_type=f32)
+    up_grad = jax.vjp(gelu_exact, saved["up"])[1](active_grad)[0].astype(jnp.bfloat16)
+    d_down = jnp.einsum("tf,td->fd", saved["active"], g, preferred_element_type=f32)
+    d_up = jnp.einsum("td,tf->df", saved["mlp_in"], up_grad, preferred_element_type=f32)
+    mlp_in_grad = jnp.einsum("tf,df->td", up_grad, w["up"], preferred_element_type=f32)
+    mixed_grad = jnp.einsum("td,fd->tf", g, w["out"], preferred_element_type=f32)
+    mixed_grad = mixed_grad.astype(jnp.bfloat16)
+    d_out = jnp.einsum("tf,td->fd", saved["mixed"], g, preferred_element_type=f32)
+    rows, width = mixed_grad.shape
+    heads = width // HD
+    q = saved["q"].reshape(rows, heads, HD)
+    mg = mixed_grad.reshape(rows, heads, HD)
+    prob = saved["prob"]
+    prob_grad = jnp.einsum("qhd,khd->hqk", mg, saved["values"], preferred_element_type=f32)
+    delta = jnp.sum(prob * prob_grad, axis=-1, keepdims=True)
+    score_grad = (prob * (prob_grad - delta) * (1.0 / math.sqrt(HD))).astype(jnp.bfloat16)
+    dq = jnp.einsum("hqk,khd->qhd", score_grad, saved["keys"], preferred_element_type=f32)
+    dk = jnp.einsum("hqk,qhd->khd", score_grad, q, preferred_element_type=f32)
+    dv = jnp.einsum("hqk,qhd->khd", prob.astype(jnp.bfloat16), mg, preferred_element_type=f32)
+    dkv = jnp.stack([dk.reshape(-1, width), dv.reshape(-1, width)])
+    dkv = dkv[:, :rows] + swapped(dkv[:, rows:], CORE)
+    dq = turn(dq.reshape(rows, width), cosine, -sine)
+    dk = turn(dkv[0], cosine, -sine)
+    qkv_grad = jnp.stack([dq, dk, dkv[1]]).astype(jnp.bfloat16)
+    attn_in_grad = jnp.einsum("ctf,cdf->td", qkv_grad, w["qkv"], preferred_element_type=f32)
+    d_qkv = jnp.einsum("td,ctf->cdf", saved["attn_in"], qkv_grad, preferred_element_type=f32)
+    normed = saved["normed"]
+    small = dict(
+        lines=[
+            jnp.sum(attn_in_grad * normed, axis=0),
+            jnp.sum(attn_in_grad, axis=0),
+            jnp.sum(mlp_in_grad * normed, axis=0),
+            jnp.sum(mlp_in_grad, axis=0),
+        ],
+        qkv=jnp.sum(qkv_grad.astype(f32), axis=1),
+        up=jnp.sum(up_grad.astype(f32), axis=0),
+        branch=jnp.sum(g.astype(f32), axis=0),
+    )
+    dn = attn_in_grad * w["gains"][0] + mlp_in_grad * w["gains"][2]
+    return dn, dict(qkv=d_qkv, up=d_up, out=d_out, down=d_down), small
+
+
+def scatter_sum(partial, at):
+    rows = partial.shape[0] // 8
+    pieces = partial.astype(jnp.bfloat16).reshape(8, rows, partial.shape[1])
+    total = part(partial, at.chip, rows, 0)
+    got = [swapped(pick(pieces, at.chip ^ j), CHIPS[j]) for j in range(1, 8)]
+    for piece in got:
+        total = total + piece.astype(jnp.float32)
+    return total
+
+
+def gather_rows(piece, at):
+    got = [piece] + [swapped(piece, CHIPS[j]) for j in range(1, 8)]
+    return in_order(got, at.chip).reshape(-1, piece.shape[1])
+
+
+def spread_rows(full, at):
+    blocks = full.reshape(4, -1, full.shape[1])
+    mine = pick(blocks, 2 * at.half + at.near)
+    got = swapped(pick(blocks, 2 * (1 - at.half) + at.near), HALF)
+    return jnp.where(at.half == 0, jnp.stack([mine, got]), jnp.stack([got, mine]))
+
+
+def deliver_rows(piece, layer, at):
+    got = swapped(piece, SECTION)
+    both = jnp.where(at.section == 0, jnp.stack([piece, got]), jnp.stack([got, piece]))
+    rest = swapped(both, SIDE)
+    low = jnp.where(at.side == 0, both, rest)
+    high = jnp.where(at.side == 0, rest, both)
+    blocks = jnp.concatenate([low, high], axis=1)
+    mine = pick(blocks, at.half)
+    got = swapped(pick(blocks, 1 - at.half), HALF)
+    return jnp.where(at.half == 0, jnp.stack([mine, got]), jnp.stack([got, mine]))
+
+
+def matrix_grads(grads, layer, at):
+    f32, b16 = jnp.float32, jnp.bfloat16
+
+    def reduce(array, axis, join):
+        shape = array.shape
+        cut = shape[:axis] + (2, 2, 2, shape[axis] // 8) + shape[axis + 1 :]
+        array = array.reshape(cut)
+        give = pick(array, 1 - at.core, axis + 2).astype(b16)
+        array = pick(array, at.core, axis + 2) + swapped(give, CORE).astype(f32)
+        give = pick(array, 1 - at.half, axis).astype(b16)
+        array = pick(array, at.half, axis) + swapped(give, HALF).astype(f32)
+        array = array.astype(b16)
+        mine = pick(array, at.near, axis)
+        give = pick(array, 1 - at.near, axis)
+        near = swapped(give, NEAR, lambda i: i // 16 == layer)
+        far = swapped(mine, SECTION, lambda i: i // 16 != layer)
+        cross = swapped(give, SECTION | NEAR, lambda i: i // 16 != layer)
+        first = [jnp.where(at.near == 0, mine, near), jnp.where(at.near == 0, near, mine)]
+        second = [jnp.where(at.near == 0, far, cross), jnp.where(at.near == 0, cross, far)]
+        order = first + second if layer == 0 else second + first
+        return jnp.concatenate(order, axis=join)
+
+    return dict(
+        qkv=reduce(grads["qkv"], 1, 2),
+        up=reduce(grads["up"], 0, 1),
+        out=reduce(grads["out"], 1, 0),
+        down=reduce(grads["down"], 1, 0),
+    )
+
+
+def vector_grads(small, at, tp_parts):
+    index = 2 * at.section + at.near
+    f32 = jnp.float32
+
+    def placed(array, axis):
+        size = array.shape[axis]
+        shape = array.shape[:axis] + (size * 4 * tp_parts,) + array.shape[axis + 1 :]
+        return lax.dynamic_update_slice_in_dim(
+            jnp.zeros(shape, f32), array, (at.side * 4 + index) * size, axis
+        )
+
+    branch = jnp.where(at.chip == 0, small["branch"], 0.0)
+    qkv = placed(small["qkv"], 1)
+    up = placed(small["up"], 0)
+    packed = jnp.concatenate(small["lines"] + [branch, qkv.reshape(-1), up])
+    packed = lax.psum(packed, ALL)
+    dim = branch.shape[0]
+    lines = [packed[i * dim : (i + 1) * dim] for i in range(5)]
+    qkv = packed[5 * dim : 5 * dim + qkv.size].reshape(qkv.shape)
+    up = packed[5 * dim + qkv.size :]
+    return lines, part(qkv, at.side, qkv.shape[1] // tp_parts, 1), part(
+        up, at.side, up.shape[0] // tp_parts, 0
+    )
+
+
+def cube_device(
+    inputs, cotangent, ln1_gain, ln1_bias, ln2_gain, ln2_bias, qkv_weight, qkv_bias,
+    out_weight, up_weight, up_bias, down_weight, branch_bias,
+):
+    at = Place()
+    rows = inputs.shape[1]
+    x = gather_start(inputs, at)
+    layers = shard_weights(
+        (
+            (ln1_gain[0], ln1_bias[0], ln2_gain[0], ln2_bias[0]),
+            qkv_weight[0], qkv_bias[0], out_weight[0], up_weight[0], up_bias[0],
+            down_weight[0], branch_bias[0],
+        ),
+        at,
+    )
+    g = gather_start(cotangent, at)
+    dim = inputs.shape[2]
+    x = x.reshape(-1, dim)
+    g = g.reshape(-1, dim)
+    place = jnp.arange(4 * rows, dtype=jnp.int32)
+    own_pos = (2 * (place // rows) + at.core) * rows + place % rows
+    other_pos = (2 * (place // rows) + 1 - at.core) * rows + place % rows
+    cosine, sine = tables(own_pos)
+    eighth = 4 * rows // 8
+
+    partial, saved_first = forward_part(x, layers[0], own_pos, other_pos, cosine, sine)
+    total = scatter_sum(partial, at)
+    x_piece = part(x, at.chip, eighth, 0).astype(jnp.float32)
+    piece = (x_piece + total + layers[0]["branch"]).astype(jnp.bfloat16)
+    middle = gather_rows(piece, at)
+    acts_first = spread_rows(middle, at)
+
+    partial, saved_second = forward_part(middle, layers[1], own_pos, other_pos, cosine, sine)
+    total = scatter_sum(partial, at)
+    last = (piece.astype(jnp.float32) + total + layers[1]["branch"]).astype(jnp.bfloat16)
+    acts_second = deliver_rows(last, 1, at)
+
+    def input_grad(dn, g_piece, x_piece):
+        total = scatter_sum(dn, at)
+        normed, scale = normal(x_piece)
+        inner = (
+            total
+            - jnp.mean(total, axis=-1, keepdims=True)
+            - normed * jnp.mean(total * normed, axis=-1, keepdims=True)
+        )
+        return (g_piece.astype(jnp.float32) + scale * inner).astype(jnp.bfloat16)
+
+    dn, grads_second, small_second = backward_part(g, saved_second, layers[1], cosine, sine)
+    g_piece = input_grad(dn, part(g, at.chip, eighth, 0), piece)
+    g_middle = gather_rows(g_piece, at)
+    in_second = spread_rows(g_middle, at)
+    done_second = matrix_grads(grads_second, 1, at)
+    vectors_second = vector_grads(small_second, at, 2)
+
+    dn, grads_first, small_first = backward_part(g_middle, saved_first, layers[0], cosine, sine)
+    g_last = input_grad(dn, g_piece, part(x, at.chip, eighth, 0))
+    in_first = deliver_rows(g_last, 0, at)
+    done_first = matrix_grads(grads_first, 0, at)
+    vectors_first = vector_grads(small_first, at, 2)
+
+    def choose(a, b):
+        return jnp.where(at.section == 0, a, b)[None]
+
+    def matrix(name):
+        return choose(done_first[name], done_second[name]).astype(jnp.float32)
+
+    lines = [choose(a, b) for a, b in zip(vectors_first[0], vectors_second[0])]
+    return (
+        choose(acts_first, acts_second),
+        choose(in_first, in_second),
+        lines[0],
+        lines[1],
+        lines[2],
+        lines[3],
+        matrix("qkv"),
+        choose(vectors_first[1], vectors_second[1]),
+        matrix("out"),
+        matrix("up"),
+        choose(vectors_first[2], vectors_second[2]),
+        matrix("down"),
+        lines[4],
+    )
+
+
+def placed_program(mesh, device_program):
     placed = (
         P(None, "ctx", None),
         P(None, "ctx", None),
@@ -325,7 +708,7 @@
         P("section", None),
     )
     return jax.shard_map(
-        per_device,
+        device_program,
         mesh=mesh,
         in_specs=placed,
         out_specs=(
@@ -345,3 +728,10 @@
         ),
         check_vma=False,
     )
+
+
+def solution(mesh):
+    sizes = dict(mesh.shape)
+    if sizes["section"] == 2 and sizes["tp"] == 2 and sizes["ctx"] == 8:
+        return placed_program(mesh, cube_device)
+    return placed_program(mesh, per_device)

time: 908 us -> 677 us (0.75)
  waiting for transfers between devices: 460 us -> 229 us
  starting transfers between devices: 11.7 us -> 149 us
  local copies, waits for them, and re-layouts: 147 us -> 79.4 us
  blocking collectives: 31.7 us -> 0 us
  matrix products: 150 us -> 128 us
  other arithmetic: 80.8 us -> 65 us
    reduce_scatter x7 -> x0, waiting for transfers between devices: 152 us -> none  [the longest x3 80.8 us: backward_layer(): lax.psum_scatter(value_terms.reshape(key_count, feat_width), 'ctx', scatt...]
    ppermute x4 -> x111, starting transfers between devices: 9.83 us -> 149 us  [swapped(): return lax.ppermute(array, ALL, pairs)]
    ppermute x4 -> x111, waiting for transfers between devices: 26.5 us -> 128 us  [swapped(): return lax.ppermute(array, ALL, pairs)]
    all_gather x6 -> x0, waiting for transfers between devices: 95.3 us -> none  [the longest x3 50.3 us: forward_layer(): lax.all_gather(value_flat, 'ctx', axis=0, tiled=True)]
    unnamed x283 -> x326, local copies, waits for them, and re-layouts: 88.6 us -> 13.2 us
    unnamed x24 -> x1, waiting for transfers between devices: 48.3 us -> 0.02 us
    psum x5 -> x1, waiting for transfers between devices: 137 us -> 101 us  [vector_grads(): packed = lax.psum(packed, ALL)]
    psum x1 -> x0, blocking collectives: 31.7 us -> none  [per_device(): lax.psum(gain_one_grad[None].astype(jnp.bfloat16), 'ctx')]
  transfers between devices with their start and end apart: 25 -> 112, of which waited for: 23 -> 38; matrix products, arithmetic and copies ran while one was open for 28% -> 37% of each run, Pallas kernels for 0% -> 0%
where the time goes in v1:
time: 677 us; the launch traced here: 669 us
  waiting for transfers between devices  229 us (34%)
  starting transfers between devices  149 us (22%)
  matrix products  128 us (19%)
  local copies, waits for them, and re-layouts  79.4 us (12%)
  other arithmetic  65 us (10%)
  between operations  17.8 us (3%)
    ppermute x111, starting transfers between devices, swapped(): return lax.ppermute(array, ALL, pairs)  149 us
    ppermute x111, waiting for transfers between devices, swapped(): return lax.ppermute(array, ALL, pairs)  128 us
    psum x1, waiting for transfers between devices, vector_grads(): packed = lax.psum(packed, ALL)  101 us
    dot_general x2, matrix products, backward_part(): jnp.einsum('hqk,khd->qhd', score_grad, saved['keys'], preferred_element_t...  24.2 us
    dot_general x2, matrix products, backward_part(): dk = jnp.einsum('hqk,qhd->khd', score_grad, q, preferred_element_type=f32)  22.6 us
  transfers between devices with their start and end apart: 112, of which 38 were waited for; matrix products, arithmetic and copies ran while one was open for 37% of the time, Pallas kernels for 0%

profile of v1, /device:TPU:0, one launch (start us, length us, event | category | flops | bytes accessed | tf_op | source)
XLA Modules:
  0.0 668.5 jit_solution(4384263401874345485)
XLA Ops:
  8.3 5.1 collective-permute-start.41
  50.0 3.2 collective-permute-done.2
  55.7 5.4 collective-permute-done.43
  77.9 6.0 multiply_convert_fusion.3
  83.8 5.3 fusion.302
  89.2 3.1 convolution_convert_fusion.1
  108.2 4.0 collective-permute-done.18
  122.4 3.9 collective-permute-done.27
  147.0 7.4 %multiply_convert_fusion.2 = (bf16[512,512]{1,0:T(8,128)(2,1)S(1)}, f32[512,512]{1,0:T(8,128)S(1)}, f32[512,512]{1,0:T(8,128)S(1)}) fusion(f32[512]{0:T(512)S(1)} %bitcast.782, bf16[512,1024]{1,0:T(8,128)(2,1)S(1)} %bitcast.688, pred[]{:T(512)S(6)} %eq.23, bf16[1,512,512]{2,1,0:T(8,128)(2,1)S(1)} %bitcast.714, bf16[1,512,512]{2,1,0:T(8,128)(2,1)S(1)} %bitcast.712, ...), kind=kOutput, calls=%fused_computation.133 | convolution fusion | flops 556793856 | bytes 5769221 | tf_op jit(solution)/shard_map/dot_general | solution.py:465
  157.9 3.1 convert_reduce_fusion.4
  163.2 2.8 fusion.306
  166.0 3.7 fusion.304
  169.7 2.9 fusion.94
  174.9 11.3 %fusion.13 = f32[2,64,1024]{2,1,0:T(8,128)S(1)} fusion(f32[2,512,1024]{2,1,0:T(8,128)} %fusion.306, bf16[512,2,48]{0,2,1:T(8,128)(2,1)S(1)} %copy-done.99, bf16[512,2,8]{0,2,1:T(8,128)(2,1)S(1)} %copy-done.127, bf16[512,2,8]{0,2,1:T(8,128)(2,1)S(1)} %copy-done.126, f32[2,512,1024]{2,1,0:T(8,128)} %get-tuple-element.244, f32[2,512]{1,0:T(2,128)S(1)} %get-tuple-element.243), kind=kOutput, calls=%fused_computation.18 | convolution fusion | flops 141953024 | bytes 9048064 | tf_op jit(solution)/shard_map/hqk,qhd->khd/dot_general | solution.py:496
  190.7 12.0 %fusion.53 = f32[512,2,64]{0,2,1:T(8,128)} fusion(bf16[1024,2,64]{0,2,1:T(8,128)(2,1)} %bitcast.750, f32[2,512,1024]{2,1,0:T(8,128)} %fusion.306, f32[2,512,1024]{2,1,0:T(8,128)} %get-tuple-element.244, f32[2,512]{1,0:T(2,128)} %copy-done.152), kind=kOutput, calls=%fused_computation.79 | convolution fusion | flops 141559808 | bytes 8916992 | tf_op jit(solution)/shard_map/hqk,khd->qhd/dot_general | solution.py:495
  205.5 3.9 fusion.305
  212.9 5.7 collective-permute-start.89
  224.3 11.5 %collective-permute-done.107 = bf16[512,2,128]{2,0,1:T(8,128)(2,1)S(1)} collective-permute-done((bf16[512,2,128]{2,0,1:T(8,128)(2,1)S(1)}, bf16[512,2,128]{2,0,1:T(8,128)(2,1)S(1)}, u32[]{:S(2)}, u32[]{:S(2)}) %collective-permute-start.107) | collective-permute-done | bytes 262176 | tf_op jit(solution)/shard_map/ppermute | solution.py:318
  243.4 5.7 fusion.284
  258.1 2.9 collective-permute-start.48
  264.4 3.3 copy.67
  287.1 3.0 collective-permute-start.109
  304.0 3.3 collective-permute-start.28
  307.3 2.5 collective-permute-done.55
  315.7 2.8 fusion.307
  318.5 11.3 %fusion.19 = f32[2,64,1024]{2,1,0:T(8,128)S(1)} fusion(f32[2,512,1024]{2,1,0:T(8,128)} %fusion.307, bf16[512,2,48]{0,2,1:T(8,128)(2,1)S(1)} %copy-done.98, bf16[512,2,8]{0,2,1:T(8,128)(2,1)S(1)} %copy-done.125, bf16[512,2,8]{0,2,1:T(8,128)(2,1)S(1)} %copy-done.123, f32[2,512,1024]{2,1,0:T(8,128)} %get-tuple-element.238, f32[2,512]{1,0:T(2,128)S(1)} %copy-done.151), kind=kOutput, calls=%fused_computation.20 | convolution fusion | flops 141953024 | bytes 9048064 | tf_op jit(solution)/shard_map/hqk,qhd->khd/dot_general | solution.py:496
  329.8 12.2 %fusion.50 = f32[512,2,64]{0,2,1:T(8,128)} fusion(bf16[1024,2,64]{0,2,1:T(8,128)(2,1)S(1)} %bitcast.745, f32[2,512,1024]{2,1,0:T(8,128)} %fusion.307, f32[2,512,1024]{2,1,0:T(8,128)} %get-tuple-element.238, f32[2,512]{1,0:T(2,128)S(1)} %copy-done.151), kind=kOutput, calls=%fused_computation.78 | convolution fusion | flops 141559808 | bytes 8916992 | tf_op jit(solution)/shard_map/hqk,khd->qhd/dot_general | solution.py:495
  349.3 3.7 convert_reduce_fusion.5
  361.8 4.5 collective-permute-done.82
  368.6 3.6 collective-permute-done.83
  382.9 12.7 %collective-permute-done.77 = bf16[3,2,128,128]{3,2,1,0:T(8,128)(2,1)S(1)} collective-permute-done((bf16[3,2,128,128]{3,2,1,0:T(8,128)(2,1)S(1)}, bf16[3,2,128,128]{3,2,1,0:T(8,128)(2,1)S(1)}, u32[]{:S(2)}, u32[]{:S(2)}) %collective-permute-start.77) | collective-permute-done | bytes 196640 | tf_op jit(solution)/shard_map/ppermute | solution.py:318
  399.1 13.3 %collective-permute-done.97 = bf16[2,128,512]{2,1,0:T(8,128)(2,1)S(1)} collective-permute-done((bf16[2,128,512]{2,1,0:T(8,128)(2,1)S(1)}, bf16[2,128,512]{2,1,0:T(8,128)(2,1)S(1)}, u32[]{:S(2)}, u32[]{:S(2)}) %collective-permute-start.97) | collective-permute-done | bytes 262176 | tf_op jit(solution)/shard_map/ppermute | solution.py:318
  412.4 7.3 %collective-permute-start.79 = (bf16[3,128,128]{2,1,0:T(8,128)(2,1)}, bf16[3,128,128]{2,1,0:T(8,128)(2,1)}, u32[]{:S(2)}, u32[]{:S(2)}) collective-permute-start(bf16[3,128,128]{2,1,0:T(8,128)(2,1)} %dynamic-slice_bitcast_fusion.48), channel_id=1, source_target_pairs={{0,20},{1,21},{2,22},{3,23},{4,16},{5,17},{6,18},{7,19},{8,28},{9,... | collective-permute-start | bytes 294920 | tf_op jit(solution)/shard_map/ppermute | solution.py:318
  420.5 2.7 collective-permute-start.78
  431.9 4.4 fusion.283
  439.9 2.8 reshape.1578
  458.8 3.0 copy.64
  461.8 2.9 copy.91
  464.7 101.4 %all-reduce.3.cloned.1.call-done = (f32[12288]{0:T(1024)}, f32[12288]{0:T(1024)}) async-done(((f32[12288]{0:T(1024)}, f32[12288]{0:T(1024)}), (f32[12288]{0:T(1024)}, f32[12288]{0:T(1024)})) %all-reduce.3.cloned.1.call-update) | async-done | bytes 98320 | tf_op jit(solution)/shard_map/psum | solution.py:600
  574.2 4.2 collective-permute-start.62
  582.1 4.3 collective-permute-start.99
  590.2 14.0 %collective-permute-done.102 = bf16[512,2,128]{2,0,1:T(8,128)(2,1)S(1)} collective-permute-done((bf16[512,2,128]{2,0,1:T(8,128)(2,1)}, bf16[512,2,128]{2,0,1:T(8,128)(2,1)S(1)}, u32[]{:S(2)}, u32[]{:S(2)}) %collective-permute-start.102) | collective-permute-done | bytes 262176 | tf_op jit(solution)/shard_map/ppermute | solution.py:318
  604.2 3.2 collective-permute-start.98
  607.5 2.6 collective-permute-done.98
  613.8 3.1 collective-permute-done.103
  625.9 8.4 %collective-permute-done.72 = bf16[3,2,128,128]{3,2,1,0:T(8,128)(2,1)S(1)} collective-permute-done((bf16[3,2,128,128]{3,2,1,0:T(8,128)(2,1)S(1)}, bf16[3,2,128,128]{3,2,1,0:T(8,128)(2,1)S(1)}, u32[]{:S(2)}, u32[]{:S(2)}) %collective-permute-start.72) | collective-permute-done | bytes 196640 | tf_op jit(solution)/shard_map/ppermute | solution.py:318
  646.8 3.8 collective-permute-done.69
  654.8 5.5 collective-permute-done.94
  (788 shorter events, 292.2 us)
Async XLA Ops:
  7.2 558.9 %all-reduce.3.cloned.1.call-start = ((), (), s32[]{:S(2)}) async-start(), calls=%async_computation | async-start | bytes 196608 | tf_op jit(solution)/shard_map/psum | solution.py:600
  8.3 30.1 %collective-permute-start.41 = (bf16[128,512]{1,0:T(8,128)(2,1)S(1)}, bf16[128,512]{1,0:T(8,128)(2,1)S(1)}, u32[]{:S(2)}, u32[]{:S(2)}) collective-permute-start(bf16[128,512]{1,0:T(8,128)(2,1)S(1)} %dynamic-slice_bitcast_fusion.31), channel_id=1, source_target_pairs={{0,12},{1,13},{2,14},{3,15},{4,8},{5,9},{6,10},{7,11},{8,4},{9,5},... | collective-permute-start | bytes 393224 | tf_op jit(solution)/shard_map/ppermute | solution.py:318
  13.4 26.4 %collective-permute-start.40 = (bf16[128,512]{1,0:T(8,128)(2,1)S(1)}, bf16[128,512]{1,0:T(8,128)(2,1)S(1)}, u32[]{:S(2)}, u32[]{:S(2)}) collective-permute-start(bf16[128,512]{1,0:T(8,128)(2,1)S(1)} %dynamic-slice_bitcast_fusion.31), channel_id=1, source_target_pairs={{0,8},{1,9},{2,10},{3,11},{4,12},{5,13},{6,14},{7,15},{8,0},{9,1},... | collective-permute-start | bytes 393224 | tf_op jit(solution)/shard_map/ppermute | solution.py:318
  14.4 26.7 %collective-permute-start.1 = (bf16[128,512]{1,0:T(8,128)(2,1)S(1)}, bf16[128,512]{1,0:T(8,128)(2,1)S(1)}, u32[]{:S(2)}, u32[]{:S(2)}) collective-permute-start(bf16[128,512]{1,0:T(8,128)(2,1)S(1)} %dynamic-slice_bitcast_fusion.47), channel_id=1, source_target_pairs={{0,12},{1,13},{2,14},{3,15},{4,8},{5,9},{6,10},{7,11},{8,4},{9,5},... | collective-permute-start | bytes 393224 | tf_op jit(solution)/shard_map/ppermute | solution.py:318
  16.4 27.1 %collective-permute-start = (bf16[128,512]{1,0:T(8,128)(2,1)S(1)}, bf16[128,512]{1,0:T(8,128)(2,1)S(1)}, u32[]{:S(2)}, u32[]{:S(2)}) collective-permute-start(bf16[128,512]{1,0:T(8,128)(2,1)S(1)} %dynamic-slice_bitcast_fusion.47), channel_id=1, source_target_pairs={{0,8},{1,9},{2,10},{3,11},{4,12},{5,13},{6,14},{7,15},{8,0},{9,1},... | collective-permute-start | bytes 393224 | tf_op jit(solution)/shard_map/ppermute | solution.py:318
  23.0 14.0 %collective-permute-start.6 = (bf16[1,6016]{1,0:T(2,128)(2,1)S(1)}, bf16[1,6016]{1,0:T(2,128)(2,1)S(1)}, u32[]{:S(2)}, u32[]{:S(2)}) collective-permute-start(bf16[1,6016]{1,0:T(2,128)(2,1)S(1)} %broadcast_in_dim.39), channel_id=1, source_target_pairs={{0,16},{1,17},{2,18},{3,19},{4,20},{5,21},{6,22},{7,23},{8,24},{9,... | collective-permute-start | bytes 36104 | tf_op jit(solution)/shard_map/ppermute | solution.py:318
  38.4 15.8 %collective-permute-start.3 = (bf16[128,1024]{1,0:T(8,128)(2,1)}, bf16[128,1024]{1,0:T(8,128)(2,1)S(1)}, u32[]{:S(2)}, u32[]{:S(2)}) collective-permute-start(bf16[128,1024]{1,0:T(8,128)(2,1)} %dynamic-slice_bitcast_fusion.8), channel_id=1, source_target_pairs={{0,4},{1,5},{2,6},{3,7},{4,0},{5,1},{6,2},{7,3},{8,12},{9,13},{10,... | collective-permute-start | bytes 786440 | tf_op jit(solution)/shard_map/ppermute | solution.py:318
  39.8 21.4 %collective-permute-start.4 = (bf16[3,512,128]{2,1,0:T(8,128)(2,1)S(1)}, bf16[3,512,128]{2,1,0:T(8,128)(2,1)S(1)}, u32[]{:S(2)}, u32[]{:S(2)}) collective-permute-start(bf16[3,512,128]{2,1,0:T(8,128)(2,1)S(1)} %dynamic-slice_bitcast_fusion.2), channel_id=1, source_target_pairs={{0,16},{1,17},{2,18},{3,19},{4,20},{5,21},{6,22},{7,23},{8,24},{9,... | collective-permute-start | bytes 1179656 | tf_op jit(solution)/shard_map/ppermute | solution.py:318
  46.8 16.7 %collective-permute-start.10 = (bf16[512,512]{1,0:T(8,128)(2,1)}, bf16[512,512]{1,0:T(8,128)(2,1)}, u32[]{:S(2)}, u32[]{:S(2)}) collective-permute-start(bf16[512,512]{1,0:T(8,128)(2,1)} %dynamic-slice_bitcast_fusion.1), channel_id=1, source_target_pairs={{0,16},{1,17},{2,18},{3,19},{4,20},{5,21},{6,22},{7,23},{8,24},{9,... | collective-permute-start | bytes 1572872 | tf_op jit(solution)/shard_map/ppermute | solution.py:318
  48.5 24.5 %collective-permute-start.12 = (bf16[256,1024]{1,0:T(8,128)(2,1)}, bf16[256,1024]{1,0:T(8,128)(2,1)}, u32[]{:S(2)}, u32[]{:S(2)}) collective-permute-start(bf16[256,1024]{1,0:T(8,128)(2,1)} %dynamic-slice_bitcast_fusion), channel_id=1, source_target_pairs={{0,16},{1,17},{2,18},{3,19},{4,20},{5,21},{6,22},{7,23},{8,24},{9,... | collective-permute-start | bytes 1572872 | tf_op jit(solution)/shard_map/ppermute | solution.py:318
  63.5 13.0 %collective-permute-start.11 = (bf16[512,512]{1,0:T(8,128)(2,1)}, bf16[512,512]{1,0:T(8,128)(2,1)}, u32[]{:S(2)}, u32[]{:S(2)}) collective-permute-start(bf16[512,512]{1,0:T(8,128)(2,1)} %collective-permute-done.10), channel_id=1, source_target_pairs={{0,2},{1,3},{2,0},{3,1},{4,6},{5,7},{6,4},{7,5},{8,10},{9,11},{10,... | collective-permute-start | bytes 1572872 | tf_op jit(solution)/shard_map/ppermute | solution.py:318
  73.0 19.8 %collective-permute-start.13 = (bf16[256,1024]{1,0:T(8,128)(2,1)}, bf16[256,1024]{1,0:T(8,128)(2,1)}, u32[]{:S(2)}, u32[]{:S(2)}) collective-permute-start(bf16[256,1024]{1,0:T(8,128)(2,1)} %collective-permute-done.12), channel_id=1, source_target_pairs={{0,2},{1,3},{2,0},{3,1},{4,6},{5,7},{6,4},{7,5},{8,10},{9,11},{10,... | collective-permute-start | bytes 1572872 | tf_op jit(solution)/shard_map/ppermute | solution.py:318
  117.8 12.9 %collective-permute-start.26 = (bf16[64,1024]{1,0:T(8,128)(2,1)S(1)}, bf16[64,1024]{1,0:T(8,128)(2,1)S(1)}, u32[]{:S(2)}, u32[]{:S(2)}) collective-permute-start(bf16[64,1024]{1,0:T(8,128)(2,1)S(1)} %get-tuple-element.62), channel_id=1, source_target_pairs={{0,4},{1,5},{2,6},{3,7},{4,0},{5,1},{6,2},{7,3},{8,12},{9,13},{10,... | collective-permute-start | bytes 393224 | tf_op jit(solution)/shard_map/ppermute | solution.py:318
  146.9 15.1 %collective-permute-start.29 = (bf16[2,512,128]{1,2,0:T(8,128)(2,1)}, bf16[2,512,128]{1,2,0:T(8,128)(2,1)}, u32[]{:S(2)}, u32[]{:S(2)}) collective-permute-start(bf16[2,512,128]{1,2,0:T(8,128)(2,1)} %pad_maximum_fusion.31), channel_id=1, source_target_pairs={{0,2},{1,3},{2,0},{3,1},{4,6},{5,7},{6,4},{7,5},{8,10},{9,11},{10,... | collective-permute-start | bytes 786440 | tf_op jit(solution)/shard_map/ppermute | solution.py:318
  157.3 63.3 %collective-permute-start.106 = (bf16[512,2,2,128]{3,0,2,1:T(8,128)(2,1)}, bf16[512,2,2,128]{3,0,2,1:T(8,128)(2,1)}, u32[]{:S(2)}, u32[]{:S(2)}) collective-permute-start(bf16[512,2,2,128]{3,0,2,1:T(8,128)(2,1)} %fusion.135), channel_id=1, source_target_pairs={{0,2},{1,3},{2,0},{3,1},{4,6},{5,7},{6,4},{7,5},{8,10},{9,11},{10,... | collective-permute-start | bytes 1572872 | tf_op jit(solution)/shard_map/ppermute | solution.py:318
  187.3 50.7 %collective-permute-start.44 = (f32[2,512,128]{2,1,0:T(8,128)}, f32[2,512,128]{2,1,0:T(8,128)}, u32[]{:S(2)}, u32[]{:S(2)}) collective-permute-start(f32[2,512,128]{2,1,0:T(8,128)} %pad_maximum_fusion.17), channel_id=1, source_target_pairs={{0,2},{1,3},{2,0},{3,1},{4,6},{5,7},{6,4},{7,5},{8,10},{9,11},{10,... | collective-permute-start | bytes 1572872 | tf_op jit(solution)/shard_map/ppermute | solution.py:318
  221.9 13.9 %collective-permute-start.107 = (bf16[512,2,128]{2,0,1:T(8,128)(2,1)S(1)}, bf16[512,2,128]{2,0,1:T(8,128)(2,1)S(1)}, u32[]{:S(2)}, u32[]{:S(2)}) collective-permute-start(bf16[512,2,128]{2,0,1:T(8,128)(2,1)S(1)} %fusion.194), channel_id=1, source_target_pairs={{0,8},{1,9},{2,10},{3,11},{4,12},{5,13},{6,14},{7,15},{8,0},{9,1},... | collective-permute-start | bytes 786440 | tf_op jit(solution)/shard_map/ppermute | solution.py:318
  236.6 33.7 %collective-permute-start.110 = (bf16[512,128]{1,0:T(8,128)(2,1)}, bf16[512,128]{1,0:T(8,128)(2,1)}, u32[]{:S(2)}, u32[]{:S(2)}) collective-permute-start(bf16[512,128]{1,0:T(8,128)(2,1)} %dynamic-slice_bitcast_fusion.9), channel_id=1, source_target_pairs={{16,20},{17,21},{18,22},{19,23},{20,16},{21,17},{22,18},{23,19},{2... | collective-permute-start | bytes 393224 | tf_op jit(solution)/shard_map/ppermute | solution.py:318
  255.1 15.1 %collective-permute-start.51 = (bf16[64,1024]{1,0:T(8,128)(2,1)}, bf16[64,1024]{1,0:T(8,128)(2,1)}, u32[]{:S(2)}, u32[]{:S(2)}) collective-permute-start(bf16[64,1024]{1,0:T(8,128)(2,1)} %get-tuple-element.112), channel_id=1, source_target_pairs={{0,21},{1,20},{2,23},{3,22},{4,17},{5,16},{6,19},{7,18},{8,29},{9,... | collective-permute-start | bytes 393224 | tf_op jit(solution)/shard_map/ppermute | solution.py:318
  255.7 16.3 %collective-permute-start.50 = (bf16[64,1024]{1,0:T(8,128)(2,1)}, bf16[64,1024]{1,0:T(8,128)(2,1)}, u32[]{:S(2)}, u32[]{:S(2)}) collective-permute-start(bf16[64,1024]{1,0:T(8,128)(2,1)} %get-tuple-element.113), channel_id=1, source_target_pairs={{0,20},{1,21},{2,22},{3,23},{4,16},{5,17},{6,18},{7,19},{8,28},{9,... | collective-permute-start | bytes 393224 | tf_op jit(solution)/shard_map/ppermute | solution.py:318
  257.8 16.6 %collective-permute-start.49 = (bf16[64,1024]{1,0:T(8,128)(2,1)}, bf16[64,1024]{1,0:T(8,128)(2,1)}, u32[]{:S(2)}, u32[]{:S(2)}) collective-permute-start(bf16[64,1024]{1,0:T(8,128)(2,1)} %get-tuple-element.114), channel_id=1, source_target_pairs={{0,17},{1,16},{2,19},{3,18},{4,21},{5,20},{6,23},{7,22},{8,25},{9,... | collective-permute-start | bytes 393224 | tf_op jit(solution)/shard_map/ppermute | solution.py:318
  258.1 17.8 %collective-permute-start.48 = (bf16[64,1024]{1,0:T(8,128)(2,1)}, bf16[64,1024]{1,0:T(8,128)(2,1)}, u32[]{:S(2)}, u32[]{:S(2)}) collective-permute-start(bf16[64,1024]{1,0:T(8,128)(2,1)} %get-tuple-element.115), channel_id=1, source_target_pairs={{0,16},{1,17},{2,18},{3,19},{4,20},{5,21},{6,22},{7,23},{8,24},{9,... | collective-permute-start | bytes 393224 | tf_op jit(solution)/shard_map/ppermute | solution.py:318
  304.0 116.5 %collective-permute-start.28 = (bf16[128,1024]{1,0:T(8,128)(2,1)}, bf16[128,1024]{1,0:T(8,128)(2,1)}, u32[]{:S(2)}, u32[]{:S(2)}) collective-permute-start(bf16[128,1024]{1,0:T(8,128)(2,1)} %get-tuple-element.130), channel_id=1, source_target_pairs={{0,8},{1,9},{2,10},{3,11},{4,12},{5,13},{6,14},{7,15},{8,0},{9,1},... | collective-permute-start | bytes 786440 | tf_op jit(solution)/shard_map/ppermute | solution.py:318
  307.3 52.1 %collective-permute-start.76 = (bf16[3,2,2,128,128]{4,3,2,1,0:T(8,128)(2,1)}, bf16[3,2,2,128,128]{4,3,2,1,0:T(8,128)(2,1)}, u32[]{:S(2)}, u32[]{:S(2)}) collective-permute-start(bf16[3,2,2,128,128]{4,3,2,1,0:T(8,128)(2,1)} %bitcast.582), channel_id=1, source_target_pairs={{0,2},{1,3},{2,0},{3,1},{4,6},{5,7},{6,4},{7,5},{8,10},{9,11},{10,... | collective-permute-start | bytes 1179656 | tf_op jit(solution)/shard_map/ppermute | solution.py:318
  309.8 62.4 %collective-permute-start.96 = (bf16[2,2,128,512]{3,2,1,0:T(8,128)(2,1)}, bf16[2,2,128,512]{3,2,1,0:T(8,128)(2,1)}, u32[]{:S(2)}, u32[]{:S(2)}) collective-permute-start(bf16[2,2,128,512]{3,2,1,0:T(8,128)(2,1)} %fusion.133), channel_id=1, source_target_pairs={{0,2},{1,3},{2,0},{3,1},{4,6},{5,7},{6,4},{7,5},{8,10},{9,11},{10,... | collective-permute-start | bytes 1572872 | tf_op jit(solution)/shard_map/ppermute | solution.py:318
  309.8 32.9 %collective-permute-start.37 = (bf16[64,1024]{1,0:T(8,128)(2,1)S(1)}, bf16[64,1024]{1,0:T(8,128)(2,1)S(1)}, u32[]{:S(2)}, u32[]{:S(2)}) collective-permute-start(bf16[64,1024]{1,0:T(8,128)(2,1)S(1)} %get-tuple-element.198), channel_id=1, source_target_pairs={{0,16},{1,17},{2,18},{3,19},{4,20},{5,21},{6,22},{7,23},{8,24},{9,... | collective-permute-start | bytes 393224 | tf_op jit(solution)/shard_map/ppermute | solution.py:318
  343.5 31.3 %collective-permute-start.38 = (bf16[2,64,1024]{2,1,0:T(8,128)(2,1)}, bf16[2,64,1024]{2,1,0:T(8,128)(2,1)}, u32[]{:S(2)}, u32[]{:S(2)}) collective-permute-start(bf16[2,64,1024]{2,1,0:T(8,128)(2,1)} %maximum_select_fusion.7), channel_id=1, source_target_pairs={{0,1},{1,0},{2,3},{3,2},{4,5},{5,4},{6,7},{7,6},{8,9},{9,8},{10,11... | collective-permute-start | bytes 786440 | tf_op jit(solution)/shard_map/ppermute | solution.py:318
  358.4 67.5 %collective-permute-start.59 = (f32[2,512,128]{2,1,0:T(8,128)}, f32[2,512,128]{2,1,0:T(8,128)S(1)}, u32[]{:S(2)}, u32[]{:S(2)}) collective-permute-start(f32[2,512,128]{2,1,0:T(8,128)} %pad_maximum_fusion.16), channel_id=1, source_target_pairs={{0,2},{1,3},{2,0},{3,1},{4,6},{5,7},{6,4},{7,5},{8,10},{9,11},{10,... | collective-permute-start | bytes 1572872 | tf_op jit(solution)/shard_map/ppermute | solution.py:318
  372.2 78.7 %collective-permute-start.101 = (bf16[512,2,2,128]{3,0,2,1:T(8,128)(2,1)}, bf16[512,2,2,128]{3,0,2,1:T(8,128)(2,1)}, u32[]{:S(2)}, u32[]{:S(2)}) collective-permute-start(bf16[512,2,2,128]{3,0,2,1:T(8,128)(2,1)} %fusion.134), channel_id=1, source_target_pairs={{0,2},{1,3},{2,0},{3,1},{4,6},{5,7},{6,4},{7,5},{8,10},{9,11},{10,... | collective-permute-start | bytes 1572872 | tf_op jit(solution)/shard_map/ppermute | solution.py:318
  378.9 16.7 %collective-permute-start.77 = (bf16[3,2,128,128]{3,2,1,0:T(8,128)(2,1)S(1)}, bf16[3,2,128,128]{3,2,1,0:T(8,128)(2,1)S(1)}, u32[]{:S(2)}, u32[]{:S(2)}) collective-permute-start(bf16[3,2,128,128]{3,2,1,0:T(8,128)(2,1)S(1)} %fusion.220), channel_id=1, source_target_pairs={{0,8},{1,9},{2,10},{3,11},{4,12},{5,13},{6,14},{7,15},{8,0},{9,1},... | collective-permute-start | bytes 589832 | tf_op jit(solution)/shard_map/ppermute | solution.py:318
  380.6 42.6 %collective-permute-start.39 = (bf16[128,1024]{1,0:T(8,128)(2,1)S(1)}, bf16[128,1024]{1,0:T(8,128)(2,1)S(1)}, u32[]{:S(2)}, u32[]{:S(2)}) collective-permute-start(bf16[128,1024]{1,0:T(8,128)(2,1)S(1)} %get-tuple-element.158), channel_id=1, source_target_pairs={{0,8},{1,9},{2,10},{3,11},{4,12},{5,13},{6,14},{7,15},{8,0},{9,1},... | collective-permute-start | bytes 786440 | tf_op jit(solution)/shard_map/ppermute | solution.py:318
  397.7 14.6 %collective-permute-start.97 = (bf16[2,128,512]{2,1,0:T(8,128)(2,1)S(1)}, bf16[2,128,512]{2,1,0:T(8,128)(2,1)S(1)}, u32[]{:S(2)}, u32[]{:S(2)}) collective-permute-start(bf16[2,128,512]{2,1,0:T(8,128)(2,1)S(1)} %fusion.192), channel_id=1, source_target_pairs={{0,8},{1,9},{2,10},{3,11},{4,12},{5,13},{6,14},{7,15},{8,0},{9,1},... | collective-permute-start | bytes 786440 | tf_op jit(solution)/shard_map/ppermute | solution.py:318
  412.4 42.2 %collective-permute-start.79 = (bf16[3,128,128]{2,1,0:T(8,128)(2,1)}, bf16[3,128,128]{2,1,0:T(8,128)(2,1)}, u32[]{:S(2)}, u32[]{:S(2)}) collective-permute-start(bf16[3,128,128]{2,1,0:T(8,128)(2,1)} %dynamic-slice_bitcast_fusion.48), channel_id=1, source_target_pairs={{0,20},{1,21},{2,22},{3,23},{4,16},{5,17},{6,18},{7,19},{8,28},{9,... | collective-permute-start | bytes 294920 | tf_op jit(solution)/shard_map/ppermute | solution.py:318
  420.5 34.6 %collective-permute-start.78 = (bf16[3,128,128]{2,1,0:T(8,128)(2,1)}, bf16[3,128,128]{2,1,0:T(8,128)(2,1)}, u32[]{:S(2)}, u32[]{:S(2)}) collective-permute-start(bf16[3,128,128]{2,1,0:T(8,128)(2,1)} %get-tuple-element.42), channel_id=1, source_target_pairs={{0,16},{1,17},{2,18},{3,19},{4,20},{5,21},{6,22},{7,23},{8,24},{9,... | collective-permute-start | bytes 294920 | tf_op jit(solution)/shard_map/ppermute | solution.py:318
  423.2 151.0 %collective-permute-start.100 = (bf16[128,512]{1,0:T(8,128)(2,1)}, bf16[128,512]{1,0:T(8,128)(2,1)S(1)}, u32[]{:S(2)}, u32[]{:S(2)}) collective-permute-start(bf16[128,512]{1,0:T(8,128)(2,1)} %dynamic-slice_bitcast_fusion.13), channel_id=1, source_target_pairs={{16,20},{17,21},{18,22},{19,23},{20,16},{21,17},{22,18},{23,19},{2... | collective-permute-start | bytes 393224 | tf_op jit(solution)/shard_map/ppermute | solution.py:318
  437.3 142.1 %collective-permute-start.66 = (bf16[64,1024]{1,0:T(8,128)(2,1)}, bf16[64,1024]{1,0:T(8,128)(2,1)S(1)}, u32[]{:S(2)}, u32[]{:S(2)}) collective-permute-start(bf16[64,1024]{1,0:T(8,128)(2,1)} %get-tuple-element.105), channel_id=1, source_target_pairs={{0,21},{1,20},{2,23},{3,22},{4,17},{5,16},{6,19},{7,18},{8,29},{9,... | collective-permute-start | bytes 393224 | tf_op jit(solution)/shard_map/ppermute | solution.py:318
  450.9 128.6 %collective-permute-start.65 = (bf16[64,1024]{1,0:T(8,128)(2,1)}, bf16[64,1024]{1,0:T(8,128)(2,1)}, u32[]{:S(2)}, u32[]{:S(2)}) collective-permute-start(bf16[64,1024]{1,0:T(8,128)(2,1)} %get-tuple-element.106), channel_id=1, source_target_pairs={{0,20},{1,21},{2,22},{3,23},{4,16},{5,17},{6,18},{7,19},{8,28},{9,... | collective-permute-start | bytes 393224 | tf_op jit(solution)/shard_map/ppermute | solution.py:318
  454.5 125.6 %collective-permute-start.64 = (bf16[64,1024]{1,0:T(8,128)(2,1)}, bf16[64,1024]{1,0:T(8,128)(2,1)}, u32[]{:S(2)}, u32[]{:S(2)}) collective-permute-start(bf16[64,1024]{1,0:T(8,128)(2,1)} %get-tuple-element.107), channel_id=1, source_target_pairs={{0,17},{1,16},{2,19},{3,18},{4,21},{5,20},{6,23},{7,22},{8,25},{9,... | collective-permute-start | bytes 393224 | tf_op jit(solution)/shard_map/ppermute | solution.py:318
  455.2 127.0 %collective-permute-start.63 = (bf16[64,1024]{1,0:T(8,128)(2,1)}, bf16[64,1024]{1,0:T(8,128)(2,1)}, u32[]{:S(2)}, u32[]{:S(2)}) collective-permute-start(bf16[64,1024]{1,0:T(8,128)(2,1)} %get-tuple-element.108), channel_id=1, source_target_pairs={{0,16},{1,17},{2,18},{3,19},{4,20},{5,21},{6,22},{7,23},{8,24},{9,... | collective-permute-start | bytes 393224 | tf_op jit(solution)/shard_map/ppermute | solution.py:318
  580.1 65.4 %collective-permute-start.70 = (bf16[128,1024]{1,0:T(8,128)(2,1)}, bf16[128,1024]{1,0:T(8,128)(2,1)S(1)}, u32[]{:S(2)}, u32[]{:S(2)}) collective-permute-start(bf16[128,1024]{1,0:T(8,128)(2,1)} %get-tuple-element.103), channel_id=1, source_target_pairs={{0,8},{1,9},{2,10},{3,11},{4,12},{5,13},{6,14},{7,15},{8,0},{9,1},... | collective-permute-start | bytes 786440 | tf_op jit(solution)/shard_map/ppermute | solution.py:318
  582.1 25.3 %collective-permute-start.99 = (bf16[128,512]{1,0:T(8,128)(2,1)}, bf16[128,512]{1,0:T(8,128)(2,1)S(1)}, u32[]{:S(2)}, u32[]{:S(2)}) collective-permute-start(bf16[128,512]{1,0:T(8,128)(2,1)} %dynamic-slice_bitcast_fusion.13), channel_id=1, source_target_pairs={{0,20},{1,21},{2,22},{3,23},{4,16},{5,17},{6,18},{7,19},{8,28},{9,... | collective-permute-start | bytes 393224 | tf_op jit(solution)/shard_map/ppermute | solution.py:318
  586.4 31.4 %collective-permute-start.71 = (bf16[3,2,2,128,128]{4,3,2,1,0:T(8,128)(2,1)}, bf16[3,2,2,128,128]{4,3,2,1,0:T(8,128)(2,1)S(1)}, u32[]{:S(2)}, u32[]{:S(2)}) collective-permute-start(bf16[3,2,2,128,128]{4,3,2,1,0:T(8,128)(2,1)} %bitcast.743), channel_id=1, source_target_pairs={{0,2},{1,3},{2,0},{3,1},{4,6},{5,7},{6,4},{7,5},{8,10},{9,11},{10,... | collective-permute-start | bytes 1179656 | tf_op jit(solution)/shard_map/ppermute | solution.py:318
  588.2 31.1 %collective-permute-start.91 = (bf16[2,2,128,512]{3,2,1,0:T(8,128)(2,1)}, bf16[2,2,128,512]{3,2,1,0:T(8,128)(2,1)S(1)}, u32[]{:S(2)}, u32[]{:S(2)}) collective-permute-start(bf16[2,2,128,512]{3,2,1,0:T(8,128)(2,1)} %fusion.132), channel_id=1, source_target_pairs={{0,2},{1,3},{2,0},{3,1},{4,6},{5,7},{6,4},{7,5},{8,10},{9,11},{10,... | collective-permute-start | bytes 1572872 | tf_op jit(solution)/shard_map/ppermute | solution.py:318
  588.2 16.0 %collective-permute-start.102 = (bf16[512,2,128]{2,0,1:T(8,128)(2,1)}, bf16[512,2,128]{2,0,1:T(8,128)(2,1)S(1)}, u32[]{:S(2)}, u32[]{:S(2)}) collective-permute-start(bf16[512,2,128]{2,0,1:T(8,128)(2,1)} %fusion.193), channel_id=1, source_target_pairs={{0,8},{1,9},{2,10},{3,11},{4,12},{5,13},{6,14},{7,15},{8,0},{9,1},... | collective-permute-start | bytes 786440 | tf_op jit(solution)/shard_map/ppermute | solution.py:318
  619.3 15.0 %collective-permute-start.72 = (bf16[3,2,128,128]{3,2,1,0:T(8,128)(2,1)S(1)}, bf16[3,2,128,128]{3,2,1,0:T(8,128)(2,1)S(1)}, u32[]{:S(2)}, u32[]{:S(2)}) collective-permute-start(bf16[3,2,128,128]{3,2,1,0:T(8,128)(2,1)S(1)} %fusion.219), channel_id=1, source_target_pairs={{0,8},{1,9},{2,10},{3,11},{4,12},{5,13},{6,14},{7,15},{8,0},{9,1},... | collective-permute-start | bytes 589832 | tf_op jit(solution)/shard_map/ppermute | solution.py:318
  621.5 21.9 %collective-permute-start.92 = (bf16[2,128,512]{2,1,0:T(8,128)(2,1)S(1)}, bf16[2,128,512]{2,1,0:T(8,128)(2,1)S(1)}, u32[]{:S(2)}, u32[]{:S(2)}) collective-permute-start(bf16[2,128,512]{2,1,0:T(8,128)(2,1)S(1)} %fusion.191), channel_id=1, source_target_pairs={{0,8},{1,9},{2,10},{3,11},{4,12},{5,13},{6,14},{7,15},{8,0},{9,1},... | collective-permute-start | bytes 786440 | tf_op jit(solution)/shard_map/ppermute | solution.py:318
  636.4 14.2 %collective-permute-start.69 = (bf16[128,1024]{1,0:T(8,128)(2,1)S(1)}, bf16[128,1024]{1,0:T(8,128)(2,1)S(1)}, u32[]{:S(2)}, u32[]{:S(2)}) collective-permute-start(bf16[128,1024]{1,0:T(8,128)(2,1)S(1)} %get-tuple-element.152), channel_id=1, source_target_pairs={{0,8},{1,9},{2,10},{3,11},{4,12},{5,13},{6,14},{7,15},{8,0},{9,1},... | collective-permute-start | bytes 786440 | tf_op jit(solution)/shard_map/ppermute | solution.py:318
  638.7 13.6 %collective-permute-start.75 = (bf16[3,128,128]{2,1,0:T(8,128)(2,1)S(1)}, bf16[3,128,128]{2,1,0:T(8,128)(2,1)S(1)}, u32[]{:S(2)}, u32[]{:S(2)}) collective-permute-start(bf16[3,128,128]{2,1,0:T(8,128)(2,1)S(1)} %dynamic-slice_bitcast_fusion.50), channel_id=1, source_target_pairs={{16,4},{17,5},{18,6},{19,7},{20,0},{21,1},{22,2},{23,3},{24,12},{2... | collective-permute-start | bytes 294920 | tf_op jit(solution)/shard_map/ppermute | solution.py:318
  (217 other events, 2028.0 us)
Sparse Core Ops, SparseCore 0:
  445.8 120.2 all-reduce.2
